TPU v7x, 32 devices: a whole 2x2x4 slice. The times are simulated.
32 devices in a mesh: rep: 8 (over z, x), shard: 4 (over y, core).
Axes of the slice: x: 2, y: 2, z: 4, core: 2. Of those that a mesh axis runs over, the one named last changes fastest.
Arguments:
- grads: bfloat16 [8, 4, 512, 3968], P('rep', 'shard'), may hold values from -6 to 6
- error: float32 [8, 512, 3968], P('rep', 'shard'), may hold values from -6 to 6
- q_factor: float32 [32, 3968], replicated, may hold values from -0.09375 to 0.09375
Outputs:
- approx: float32 [512, 3968], P('shard')
- new_error: float32 [8, 512, 3968], P('rep', 'shard')
- q_next: float32 [32, 3968], replicated
All inputs are finite; a program needn't handle non-finite values.
Results may differ from a plain program's by a relative error of at most 0.0003.
Values sent between devices are 32-bit elements; how exact they have to be, the bound alone decides.
No kernel may reach another device: no remote copies, remote signals or barrier semaphores. Data moves between devices by JAX's collectives and lax.ppermute only.
A program may use at most 128 MiB of HBM per device.

v0:
```python
import jax
import jax.numpy as jnp
from jax import lax
from jax.sharding import PartitionSpec as P


def body(grads, error, q_factor):
    local_grad = grads[0, 0].astype(jnp.float32)
    own_error = error[0]
    reduced = lax.psum_scatter(local_grad, "shard", scatter_dimension=0, tiled=True)
    merged = reduced + own_error
    factor_term = jnp.dot(
        merged, q_factor.T, precision=lax.Precision.HIGHEST, preferred_element_type=jnp.float32
    )
    own_factor = lax.psum(factor_term, "rep")
    gram_part = jnp.dot(
        own_factor.T,
        own_factor,
        precision=lax.Precision.HIGHEST,
        preferred_element_type=jnp.float32,
    )
    gram_matrix = lax.psum(gram_part, "shard")
    lower_factor = jnp.linalg.cholesky(gram_matrix)
    basis_rows = jax.scipy.linalg.solve_triangular(lower_factor, own_factor.T, lower=True)
    q_term = jnp.dot(
        basis_rows, merged, precision=lax.Precision.HIGHEST, preferred_element_type=jnp.float32
    )
    q_total_sum = lax.psum(q_term, ("rep", "shard"))
    q_next = q_total_sum / lax.axis_size("rep")
    approx = jnp.dot(
        basis_rows.T, q_next, precision=lax.Precision.HIGHEST, preferred_element_type=jnp.float32
    )
    new_error = merged - approx
    return (approx, new_error[None], q_next)


def solution(mesh):
    in_specs = (P("rep", "shard", None, None), P("rep", "shard", None), P())
    out_specs = (P("shard", None), P("rep", "shard", None), P())
    return jax.shard_map(body, mesh=mesh, in_specs=in_specs, out_specs=out_specs, check_vma=False)
```

profile of v0, /device:TPU:0, one launch (start us, length us, event | category | flops | bytes accessed | tf_op | source)
XLA Modules:
  0.0 283.3 jit_solution(12748212787060396827)
XLA Ops:
  7.2 0.0 copy-start
  7.2 0.0 reduce-scatter.2.cloned.1.call-start
  7.2 5.9 %bitcast_convert_fusion = f32[512,3968]{1,0:T(8,128)} fusion(bf16[1,1,512,3968]{3,2,1,0:T(8,128)(2,1)} %param.3), kind=kLoop, calls=%fused_computation | loop fusion | flops 2031616 | bytes 12189696 | tf_op jit(solution)/shard_map/convert_element_type | solution.py:8
  13.1 0.0 copy-start.1
  13.1 0.0 reduce-scatter.2.cloned.1.call-update
  13.1 0.0 all-reduce.2.cloned.1.call-start
  13.2 73.0 %reduce-scatter.2.cloned.1.call-done = f32[128,3968]{1,0:T(8,128)} async-done(((f32[512,3968]{1,0:T(8,128)}), f32[128,3968]{1,0:T(8,128)}) %reduce-scatter.2.cloned.1.call-update) | async-done | bytes 2031632 | tf_op jit(solution)/shard_map/reduce_scatter | solution.py:10
  86.2 0.0 copy-done
  86.2 0.0 copy-done.1
  86.2 3.6 %fusion.5 = f32[128,32]{0,1:T(8,128)S(1)} fusion(f32[32,3968]{1,0:T(8,128)S(1)} %copy-done, f32[128,3968]{1,0:T(8,128)} %reduce-scatter.2.cloned.1.call-done, f32[1,128,3968]{2,1,0:T(8,128)S(1)} %copy-done.1), kind=kOutput, calls=%fused_computation.15 | convolution fusion | flops 195543040 | bytes 4587520 | tf_op jit(solution)/shard_map/dot_general | solution.py:12
  89.8 37.1 %psum.21 = f32[128,32]{0,1:T(8,128)S(1)} all-reduce(f32[128,32]{0,1:T(8,128)S(1)} %fusion.5), channel_id=1, replica_groups=mesh['rep'=8,'shard'=4] {'rep'}, use_global_device_ids=true, to_apply=%region_1.0 | all-reduce | flops 4096 | bytes 32768 | tf_op jit(solution)/shard_map/psum | solution.py:15
  126.8 0.1 fusion.6
  127.0 10.2 %psum.22 = f32[32,32]{0,1:T(8,128)S(1)} all-reduce(f32[32,32]{0,1:T(8,128)S(1)} %fusion.6), channel_id=1, replica_groups=mesh['rep'=8,'shard'=4] {'shard'}, use_global_device_ids=true, to_apply=%region_2.0 | all-reduce | flops 1024 | bytes 8192 | tf_op jit(solution)/shard_map/psum | solution.py:22
  137.2 0.1 copy.7
  137.3 2.9 %cholesky.16 = f32[32,32]{1,0:T(8,128)S(1)} custom-call(f32[32,32]{1,0:T(8,128)S(1)} %fusion.3), custom_call_target="Cholesky" | custom-call | tf_op jit(solution)/shard_map/jit(cholesky)/cholesky | solution.py:23
  140.3 0.6 compare_reduce_fusion
  140.9 0.7 fusion
  141.6 2.5 custom-call.7
  144.0 0.2 fusion.1
  144.2 3.6 %fusion.4 = f32[32,3968]{1,0:T(8,128)} fusion(f32[32,128]{1,0:T(8,128)S(1)} %fusion.1, f32[128,3968]{1,0:T(8,128)} %reduce-scatter.2.cloned.1.call-done, f32[1,128,3968]{2,1,0:T(8,128)S(1)} %copy-done.1), kind=kOutput, calls=%fused_computation.14 | convolution fusion | flops 195543040 | bytes 4587520 | tf_op jit(solution)/shard_map/dot_general | solution.py:25
  147.9 0.0 all-reduce.2.cloned.1.call-update
  147.9 123.5 %all-reduce.2.cloned.1.call-done = f32[32,3968]{1,0:T(8,128)} async-done(((f32[32,3968]{1,0:T(8,128)}), f32[32,3968]{1,0:T(8,128)}) %all-reduce.2.cloned.1.call-update) | async-done | bytes 507920 | tf_op jit(solution)/shard_map/psum | solution.py:28
  271.4 0.0 copy-start.2
  271.4 1.2 broadcast_multiply_fusion
  272.6 0.0 copy-start.4
  272.6 1.8 fusion.7
  274.4 0.0 copy-done.2
  274.4 0.0 copy-start.3
  274.5 1.8 subtract_bitcast_fusion
  276.2 0.0 copy-done.4
  276.2 0.2 copy-done.3
  (2 shorter events, 0.0 us)
Async XLA Ops:
  7.2 79.0 %copy-start = (f32[32,3968]{1,0:T(8,128)S(1)}, f32[32,3968]{1,0:T(8,128)}, u32[]{:S(2)}) copy-start(f32[32,3968]{1,0:T(8,128)} %param.5) | copy-start | bytes 1523716
  7.2 79.0 %reduce-scatter.2.cloned.1.call-start = ((), (), s32[]{:S(2)}) async-start(), calls=%async_computation.1 | async-start | bytes 10158080 | tf_op jit(solution)/shard_map/reduce_scatter | solution.py:10
  13.1 73.1 %copy-start.1 = (f32[1,128,3968]{2,1,0:T(8,128)S(1)}, f32[1,128,3968]{2,1,0:T(8,128)}, u32[]{:S(2)}) copy-start(f32[1,128,3968]{2,1,0:T(8,128)} %param.4) | copy-start | bytes 6094852
  13.1 258.3 %all-reduce.2.cloned.1.call-start = ((), (), s32[]{:S(2)}) async-start(), calls=%async_computation.2 | async-start | bytes 1015808 | tf_op jit(solution)/shard_map/psum | solution.py:28
  271.4 3.0 %copy-start.2 = (f32[128,3968]{1,0:T(8,128)S(1)}, f32[128,3968]{1,0:T(8,128)}, u32[]{:S(2)}) copy-start(f32[128,3968]{1,0:T(8,128)} %reduce-scatter.2.cloned.1.call-done) | copy-start | bytes 6094852
  272.6 3.6 %copy-start.4 = (f32[32,3968]{1,0:T(8,128)}, f32[32,3968]{1,0:T(8,128)S(1)}, u32[]{:S(2)}) copy-start(f32[32,3968]{1,0:T(8,128)S(1)} %broadcast_multiply_fusion) | copy-start | bytes 1523716
  274.4 2.0 copy-start.3
Sparse Core Ops, SparseCore 0:
  13.3 72.8 reduce-scatter.1
  148.0 123.3 all-reduce.1
where the time goes:
time: 283 us
  waiting for transfers between devices  197 us (70%)
  blocking collectives  47.3 us (17%)
  other arithmetic  15.6 us (6%)
  between operations  14.1 us (5%)
  matrix products  9.32 us (3%)
    psum x1, waiting for transfers between devices, body(): q_total_sum = lax.psum(q_term, ('rep', 'shard'))  124 us
    reduce_scatter x1, waiting for transfers between devices, body(): lax.psum_scatter(local_grad, 'shard', scatter_dimension=0, tiled=True)  73 us
    psum x1, blocking collectives, body(): own_factor = lax.psum(factor_term, 'rep')  37.1 us
    psum x1, blocking collectives, body(): gram_matrix = lax.psum(gram_part, 'shard')  10.2 us
    convert_element_type x1, other arithmetic, body(): local_grad = grads[0, 0].astype(jnp.float32)  5.88 us
  transfers between devices with their start and end apart: 2, of which 2 were waited for; matrix products, arithmetic and copies ran while one was open for 0% of the time, Pallas kernels for 0%

commit v1 on v0

v1 whole, which is shorter than its diff:
```python
import functools

import jax
import jax.numpy as jnp
from jax import lax
from jax.experimental import pallas as pl
from jax.experimental.pallas import tpu as pltpu
from jax.sharding import PartitionSpec as P

F32 = jnp.float32
BF16 = jnp.bfloat16
LANES = 128
WIDE = 512
VMEM_LIMIT = 48 * 1024 * 1024


def pieces(x):
    high = x.astype(BF16)
    rest = x - high.astype(F32)
    mid = rest.astype(BF16)
    low = (rest - mid.astype(F32)).astype(BF16)
    return jnp.concatenate([high, mid, low], axis=0)


def fold(x, rank):
    return (x[2 * rank :] + x[rank : 2 * rank]) + x[:rank]


def dot(a, b, contract, precision=None):
    return lax.dot_general(
        a, b, (contract, ((), ())), precision=precision, preferred_element_type=F32
    )


def tree(values):
    values = list(values)
    while len(values) > 1:
        values = [values[i] + values[i + 1] for i in range(0, len(values), 2)]
    return values[0]


def params(**kw):
    return pltpu.CompilerParams(vmem_limit_bytes=VMEM_LIMIT, **kw)


def cost(flops, moved):
    return pl.CostEstimate(flops=int(flops), bytes_accessed=int(moved), transcendentals=0)


def partner(x, axis, d):
    n = lax.axis_size(axis)
    return lax.ppermute(x, axis, [(i, i ^ d) for i in range(n)])


def whole(shape):
    return pl.BlockSpec(shape, lambda *_: (0,) * len(shape))


def widen(where, grads, block_rows, first, count):
    step = 16
    cols = grads.shape[1]

    def kernel(where_ref, g_ref, o_ref):
        o_ref[...] = g_ref[...].astype(F32)

    return pl.pallas_call(
        kernel,
        out_shape=jax.ShapeDtypeStruct((count, cols), F32),
        grid_spec=pltpu.PrefetchScalarGridSpec(
            num_scalar_prefetch=1,
            grid=(count // step,),
            in_specs=[
                pl.BlockSpec(
                    (step, cols), lambda i, w: (w[0] * (block_rows // step) + first // step + i, 0)
                )
            ],
            out_specs=pl.BlockSpec((step, cols), lambda i, w: (i, 0)),
        ),
        compiler_params=params(),
        cost_estimate=cost(count * cols, 6 * count * cols),
        name="widen_rows",
    )(where, grads)


def add_rows(where, grads, arrived, block_rows, first):
    step = 16
    count, cols = arrived.shape

    def kernel(where_ref, g_ref, a_ref, o_ref):
        o_ref[...] = g_ref[...].astype(F32) + a_ref[...]

    return pl.pallas_call(
        kernel,
        out_shape=jax.ShapeDtypeStruct((count, cols), F32),
        grid_spec=pltpu.PrefetchScalarGridSpec(
            num_scalar_prefetch=1,
            grid=(count // step,),
            in_specs=[
                pl.BlockSpec(
                    (step, cols), lambda i, w: (w[0] * (block_rows // step) + first // step + i, 0)
                ),
                pl.BlockSpec((step, cols), lambda i, w: (i, 0)),
            ],
            out_specs=pl.BlockSpec((step, cols), lambda i, w: (i, 0)),
        ),
        compiler_params=params(),
        cost_estimate=cost(count * cols, 10 * count * cols),
        name="add_rows",
    )(where, grads, arrived)


def left_terms(me, grads, q_factor, n_shard):
    rows, cols = grads.shape
    block = rows // n_shard
    rank = q_factor.shape[0]

    def kernel(me_ref, g_ref, q_ref, *rest):
        outs, wide_ref, q3 = rest[:n_shard], rest[n_shard], rest[n_shard + 1]
        i = pl.program_id(0)

        @pl.when(i == 0)
        def _():
            q3[...] = pieces(q_ref[...])

        g = g_ref[...]
        term = fold(dot(q3[...], g, ((1,), (1,))), rank)
        for d in range(n_shard):

            @pl.when(i == n_shard - 1 - d)
            def _(d=d):
                outs[d][...] = term

        @pl.when(i == n_shard - 2)
        def _():
            wide_ref[...] = g.astype(F32)

    return pl.pallas_call(
        kernel,
        out_shape=[jax.ShapeDtypeStruct((rank, block), F32)] * n_shard
        + [jax.ShapeDtypeStruct((block, cols), F32)],
        grid_spec=pltpu.PrefetchScalarGridSpec(
            num_scalar_prefetch=1,
            grid=(n_shard,),
            in_specs=[
                pl.BlockSpec((block, cols), lambda i, w: (w[0] ^ (n_shard - 1 - i), 0)),
                whole((rank, cols)),
            ],
            out_specs=[whole((rank, block))] * n_shard + [whole((block, cols))],
            scratch_shapes=[pltpu.VMEM((3 * rank, cols), BF16)],
        ),
        compiler_params=params(),
        cost_estimate=cost(6 * rank * rows * cols, 2 * rows * cols + 4 * block * cols),
        name="left_terms",
    )(me, grads, q_factor)


def error_term(error, q_factor, term):
    rows, cols = error.shape
    rank = q_factor.shape[0]

    def kernel(e_ref, q_ref, t_ref, o_ref):
        q3 = pieces(q_ref[...])
        e3 = pieces(e_ref[...])
        high, mid, low = e3[:rows], e3[rows : 2 * rows], e3[2 * rows :]
        nt = ((1,), (1,))
        a = fold(dot(q3, high, nt), rank)
        b = dot(q3[: 2 * rank], mid, nt)
        c = dot(q3[:rank], low, nt)
        o_ref[...] = t_ref[...] + (a + ((b[:rank] + b[rank:]) + c))

    return pl.pallas_call(
        kernel,
        out_shape=jax.ShapeDtypeStruct((rank, rows), F32),
        compiler_params=params(),
        cost_estimate=cost(12 * rank * rows * cols, 4 * rows * cols),
        name="error_term",
    )(error, q_factor, term)


def total(*values):
    def kernel(*refs):
        refs[-1][...] = tree([r[...] for r in refs[:-1]])

    return pl.pallas_call(
        kernel,
        out_shape=jax.ShapeDtypeStruct(values[0].shape, F32),
        compiler_params=params(),
        cost_estimate=cost(0, 4 * values[0].size),
        name="total",
    )(*values)


def right_terms(me, grads, error, blocks, n_shard):
    rows, cols = grads.shape
    block = rows // n_shard
    rank = blocks[0].shape[0]
    per = WIDE // LANES
    n_wide = 2 * (-(-cols // (2 * WIDE)))
    half = n_wide // 2
    out = jax.ShapeDtypeStruct((half * per * rank, LANES), F32)

    def kernel(me_ref, g_ref, e_ref, *rest):
        b_refs = rest[:n_shard]
        send_ref, keep_ref, f_all, f3 = rest[n_shard:]
        i = pl.program_id(0)

        @pl.when(i == 0)
        def _():
            for d in range(n_shard):
                f_all[me_ref[0] ^ d] = b_refs[d][...]
            f3[...] = pieces(jnp.concatenate([f_all[j] for j in range(n_shard)], axis=1))

        value = fold(dot(f3[...], g_ref[...], ((1,), (0,))), rank)
        value += dot(b_refs[0][...], e_ref[...], ((1,), (0,)), lax.Precision.HIGHEST)
        stacked = jnp.concatenate(
            [value[:, k * LANES : (k + 1) * LANES] for k in range(per)], axis=0
        )

        @pl.when(i < half)
        def _():
            send_ref[...] = stacked

        @pl.when(i >= half)
        def _():
            keep_ref[...] = stacked

    def col(i, w):
        return (i + half * (1 - (w[0] & 1))) % n_wide

    return pl.pallas_call(
        kernel,
        out_shape=[out, out],
        grid_spec=pltpu.PrefetchScalarGridSpec(
            num_scalar_prefetch=1,
            grid=(n_wide,),
            in_specs=[
                pl.BlockSpec((rows, WIDE), lambda i, w: (0, col(i, w))),
                pl.BlockSpec((block, WIDE), lambda i, w: (0, col(i, w))),
            ]
            + [whole((rank, block))] * n_shard,
            out_specs=[
                pl.BlockSpec((per * rank, LANES), lambda i, w: (jnp.minimum(i, half - 1), 0)),
                pl.BlockSpec((per * rank, LANES), lambda i, w: (jnp.maximum(i - half, 0), 0)),
            ],
            scratch_shapes=[
                pltpu.VMEM((n_shard, rank, block), F32),
                pltpu.VMEM((3 * rank, rows), BF16),
            ],
        ),
        compiler_params=params(),
        cost_estimate=cost(6 * rank * rows * cols, 2 * rows * cols + 4 * block * cols),
        name="right_terms",
    )(me, grads, error, *blocks)


def inverse_factor(me, blocks, n_shard):
    rank, block = blocks[0].shape

    def kernel(me_ref, *rest):
        b_refs = rest[:n_shard]
        inv_ref, basis_ref, f_all = rest[n_shard:]
        for d in range(n_shard):
            f_all[me_ref[0] ^ d] = b_refs[d][...]
        f = jnp.concatenate([f_all[j] for j in range(n_shard)], axis=1)
        gram = dot(f, f, ((1,), (1,)), lax.Precision.HIGHEST)
        row = lax.broadcasted_iota(jnp.int32, (rank, 2 * rank), 0)
        col = lax.broadcasted_iota(jnp.int32, (rank, 2 * rank), 1)
        unit = jnp.where(col == row + rank, 1.0, 0.0).astype(F32)
        w = jnp.concatenate([gram, jnp.zeros_like(gram)], axis=1) + unit
        for k in range(rank):
            scale = 1.0 / jnp.sqrt(w[k : k + 1, k : k + 1])
            pivot = w[k : k + 1, :] * scale
            column = w[:, k : k + 1] * scale
            w = jnp.where(row > k, w - column * pivot, jnp.where(row == k, pivot, w))
        inverse = w[:, rank:]
        inv_ref[...] = inverse
        basis_ref[...] = dot(inverse, b_refs[0][...], ((1,), (0,)), lax.Precision.HIGHEST)

    vmem = pl.BlockSpec(memory_space=pltpu.VMEM)
    return pl.pallas_call(
        kernel,
        out_shape=[
            jax.ShapeDtypeStruct((rank, rank), F32),
            jax.ShapeDtypeStruct((rank, block), F32),
        ],
        in_specs=[pl.BlockSpec(memory_space=pltpu.SMEM)] + [vmem] * n_shard,
        out_specs=[vmem, vmem],
        scratch_shapes=[pltpu.VMEM((n_shard, rank, block), F32)],
        compiler_params=params(),
        cost_estimate=cost(rank**3 * 100, 8 * rank * block),
        name="inverse_factor",
    )(me, *blocks)


def split_sum(own, keep, arrived, n_rep):
    rows = keep.shape[0] // n_rep

    def kernel(own_ref, k_ref, a_ref, *outs):
        for d in range(n_rep):
            at = pl.ds(pl.multiple_of((own_ref[0] ^ d) * rows, rows), rows)
            outs[d][...] = k_ref[at, :] + a_ref[at, :]

    vmem = pl.BlockSpec(memory_space=pltpu.VMEM)
    return pl.pallas_call(
        kernel,
        out_shape=[jax.ShapeDtypeStruct((rows, LANES), F32)] * n_rep,
        in_specs=[pl.BlockSpec(memory_space=pltpu.SMEM), vmem, vmem],
        out_specs=[vmem] * n_rep,
        compiler_params=params(),
        cost_estimate=cost(keep.size, 12 * keep.size),
        name="split_sum",
    )(own, keep, arrived)


def join(own, parts):
    n = len(parts)
    rows = parts[0].shape[0]

    def kernel(own_ref, *refs):
        for d in range(n):
            at = pl.ds(pl.multiple_of((own_ref[0] ^ d) * rows, rows), rows)
            refs[n][at, :] = refs[d][...]

    vmem = pl.BlockSpec(memory_space=pltpu.VMEM)
    return pl.pallas_call(
        kernel,
        out_shape=jax.ShapeDtypeStruct((n * rows, LANES), F32),
        in_specs=[pl.BlockSpec(memory_space=pltpu.SMEM)] + [vmem] * n,
        out_specs=vmem,
        compiler_params=params(),
        cost_estimate=cost(0, 8 * n * rows * LANES),
        name="join",
    )(own, *parts)


def own_rows(me, grads, arrived, error, block_rows):
    step = 32
    count, cols = error.shape

    def kernel(me_ref, g_ref, a_ref, e_ref, o_ref):
        o_ref[...] = (g_ref[...].astype(F32) + a_ref[...]) + e_ref[...]

    rowwise = pl.BlockSpec((step, cols), lambda i, w: (i, 0))
    return pl.pallas_call(
        kernel,
        out_shape=jax.ShapeDtypeStruct((count, cols), F32),
        grid_spec=pltpu.PrefetchScalarGridSpec(
            num_scalar_prefetch=1,
            grid=(count // step,),
            in_specs=[
                pl.BlockSpec((step, cols), lambda i, w: (w[0] * (block_rows // step) + i, 0)),
                rowwise,
                rowwise,
            ],
            out_specs=rowwise,
        ),
        compiler_params=params(),
        cost_estimate=cost(2 * count * cols, 14 * count * cols),
        name="own_rows",
    )(me, grads, arrived, error)


def finish(core, inverse, basis, q_own, q_other, partial, arrived, n_rep):
    rows, cols = partial.shape
    rank = inverse.shape[0]
    per = WIDE // LANES
    n_wide = -(-cols // WIDE)
    half = q_own.shape[0] // (per * rank)
    counts = [a.shape[0] for a in arrived]
    n_arrived = len(arrived)

    def kernel(core_ref, inv_ref, basis_ref, own_ref, other_ref, p_ref, *rest):
        a_refs = rest[:n_arrived]
        approx_ref, error_ref, q_ref = rest[n_arrived:]
        j = pl.program_id(0)
        mine = (j // half) == core_ref[0]
        stacked = jnp.where(mine, own_ref[...], other_ref[...])
        q_sum = jnp.concatenate(
            [stacked[k * rank : (k + 1) * rank] for k in range(per)], axis=1
        )
        q_next = dot(inv_ref[...], q_sum, ((1,), (0,)), lax.Precision.HIGHEST) * (1.0 / n_rep)
        q_ref[...] = q_next
        approx = dot(basis_ref[...], q_next, ((0,), (0,)), lax.Precision.HIGHEST)
        approx_ref[...] = approx
        merged = p_ref[...]
        values = jnp.concatenate([a_ref[...] for a_ref in a_refs], axis=0)
        error_ref[...] = (merged + values) - approx

    wide = lambda r: pl.BlockSpec((r, WIDE), lambda j, c: (0, j))
    q_spec = pl.BlockSpec((per * rank, LANES), lambda j, c: (j % half, 0))
    return pl.pallas_call(
        kernel,
        out_shape=[
            jax.ShapeDtypeStruct((rows, cols), F32),
            jax.ShapeDtypeStruct((rows, cols), F32),
            jax.ShapeDtypeStruct((rank, cols), F32),
        ],
        grid_spec=pltpu.PrefetchScalarGridSpec(
            num_scalar_prefetch=1,
            grid=(n_wide,),
            in_specs=[whole(inverse.shape), whole(basis.shape), q_spec, q_spec, wide(rows)]
            + [wide(count) for count in counts],
            out_specs=[wide(rows), wide(rows), wide(rank)],
        ),
        compiler_params=params(),
        cost_estimate=cost(12 * rank * rows * cols, 16 * rows * cols),
        name="finish",
    )(core, inverse, basis, q_own, q_other, partial, *arrived)


def body(grads, error, q_factor):
    n_rep, n_shard = lax.axis_size("rep"), lax.axis_size("shard")
    grads, error = grads[0, 0], error[0]
    rows, cols = grads.shape
    block = rows // n_shard
    rank = q_factor.shape[0]
    me = lax.axis_index("shard").astype(jnp.int32)
    own = lax.axis_index("rep").astype(jnp.int32).reshape(1)
    core = (me & 1).reshape(1)
    me = me.reshape(1)

    cuts = ((0, 32), (32, 48), (80, 48))
    crossing = [[] for _ in cuts]
    for d in range(2, n_shard, 2):
        for k, (first, count) in enumerate(cuts):
            to_core = widen(me ^ (d + 1), grads, block, first, count)
            to_core = partner(to_core, "shard", 1)
            to_chip = add_rows(me ^ d, grads, to_core, block, first)
            crossing[k].append(partner(to_chip, "shard", d))
    arrived = [parts[0] if len(parts) == 1 else sum(parts) for parts in crossing]

    *terms, to_core = left_terms(me, grads, q_factor, n_shard)
    from_core = partner(to_core, "shard", 1)
    received = [partner(terms[d], "shard", d) for d in range(1, n_shard)]
    factor_part = total(error_term(error, q_factor, terms[0]), *received)
    factor_own = total(
        factor_part, *[partner(factor_part, "rep", d) for d in range(1, n_rep)]
    )
    blocks = [factor_own] + [partner(factor_own, "shard", d) for d in range(1, n_shard)]

    send, keep = right_terms(me, grads, error, blocks, n_shard)
    cut = split_sum(own, keep, partner(send, "shard", 1), n_rep)
    piece = total(cut[0], *[partner(cut[d], "rep", d) for d in range(1, n_rep)])
    piece = total(piece, *[partner(piece, "shard", d) for d in range(2, n_shard, 2)])
    q_own = join(own, [piece] + [partner(piece, "rep", d) for d in range(1, n_rep)])
    q_other = partner(q_own, "shard", 1)

    inverse, basis = inverse_factor(me, blocks, n_shard)
    partial = own_rows(me, grads, from_core, error, block)
    approx, new_error, q_next = finish(
        core, inverse, basis, q_own, q_other, partial, arrived, n_rep
    )
    return approx, new_error[None], q_next


def solution(mesh):
    in_specs = (P("rep", "shard", None, None), P("rep", "shard", None), P())
    out_specs = (P("shard", None), P("rep", "shard", None), P())
    return jax.shard_map(body, mesh=mesh, in_specs=in_specs, out_specs=out_specs, check_vma=False)
```

time: 283 us -> 150 us (0.53)
  waiting for transfers between devices: 197 us -> 53.2 us
  starting transfers between devices: 0.08 us -> 58 us
  blocking collectives: 47.3 us -> 0 us
  Pallas kernels: 0 us -> 33.8 us
  other arithmetic: 15.6 us -> 0 us
  between operations: 14.1 us -> 0.81 us
  matrix products: 9.32 us -> 0 us
  local copies, waits for them, and re-layouts: 0.29 us -> 3.2 us
    psum x1 -> x0, waiting for transfers between devices: 124 us -> none  [body(): q_total_sum = lax.psum(q_term, ('rep', 'shard'))]
    reduce_scatter x1 -> x0, waiting for transfers between devices: 73 us -> none  [body(): lax.psum_scatter(local_grad, 'shard', scatter_dimension=0, tiled=True)]
    ppermute x0 -> x37, starting transfers between devices: none -> 58 us  [partner(): return lax.ppermute(x, axis, [(i, i ^ d) for i in range(n)])]
    ppermute x0 -> x37, waiting for transfers between devices: none -> 53.2 us  [partner(): return lax.ppermute(x, axis, [(i, i ^ d) for i in range(n)])]
    psum x2 -> x0, blocking collectives: 47.3 us -> none  [the longest x1 37.1 us: body(): own_factor = lax.psum(factor_term, 'rep')]
    pallas_call x0 -> x18, Pallas kernels: none -> 33.8 us  [the longest x1 8.18 us: finish(): pl.pallas_call(kernel, out_shape=[jax.ShapeDtypeStruct((rows, cols), F32)...]
    dot_general x4 -> x0, matrix products: 9.11 us -> none  [the longest x1 3.61 us: body(): jnp.dot(basis_rows, merged, precision=lax.Precision.HIGHEST, preferred_el...]
    another operation x5 -> x0, other arithmetic: 6.71 us -> none  [the longest x3 3.59 us: body(): lower_factor = jnp.linalg.cholesky(gram_matrix)]
  transfers between devices with their start and end apart: 2 -> 37, of which waited for: 2 -> 26; matrix products, arithmetic and copies ran while one was open for 0% -> 0% of each run, Pallas kernels for 0% -> 13%
where the time goes in v1:
time: 150 us; the launch traced here: 149 us
  starting transfers between devices  58 us (39%)
  waiting for transfers between devices  53.2 us (35%)
  Pallas kernels  33.8 us (23%)
  local copies, waits for them, and re-layouts  3.2 us (2%)
    ppermute x37, starting transfers between devices, partner(): return lax.ppermute(x, axis, [(i, i ^ d) for i in range(n)])  58 us
    ppermute x37, waiting for transfers between devices, partner(): return lax.ppermute(x, axis, [(i, i ^ d) for i in range(n)])  53.2 us
    pallas_call x1, Pallas kernels, finish(): pl.pallas_call(kernel, out_shape=[jax.ShapeDtypeStruct((rows, cols), F32)...  8.18 us
    pallas_call x1, Pallas kernels, right_terms(): pl.pallas_call(kernel, out_shape=[out, out], grid_spec=pltpu.PrefetchScal...  6.9 us
    pallas_call x1, Pallas kernels, left_terms(): pl.pallas_call(kernel, out_shape=[jax.ShapeDtypeStruct((rank, block), F32...  5.62 us
    pallas_call x3, Pallas kernels, add_rows(): pl.pallas_call(kernel, out_shape=jax.ShapeDtypeStruct((count, cols), F32)...  4.68 us
    pallas_call x1, Pallas kernels, inverse_factor(): pl.pallas_call(kernel, out_shape=[jax.ShapeDtypeStruct((rank, rank), F32)...  3.42 us
    unnamed x12, local copies, waits for them, and re-layouts  3.2 us
  transfers between devices with their start and end apart: 37, of which 26 were waited for; matrix products, arithmetic and copies ran while one was open for 0% of the time, Pallas kernels for 13%

profile of v1, /device:TPU:0, one launch (start us, length us, event | category | flops | bytes accessed | tf_op | source)
XLA Modules:
  0.0 148.9 jit_solution(10455377232793601195)
XLA Ops:
  1.7 5.6 %left_terms.1 = (f32[32,128]{1,0:T(8,128)S(1)}, f32[32,128]{1,0:T(8,128)S(1)}, f32[32,128]{1,0:T(8,128)S(1)}, f32[32,128]{1,0:T(8,128)S(1)}, f32[128,3968]{1,0:T(8,128)}) custom-call(s32[1]{0:T(128)} %bitcast.1.me_ref, bf16[512,3968]{1,0:T(8,128)(2,1)} %bitcast.6, f32[32,3968]{1,0:T(8,128)S(1)} %copy-done.4), custom_call_target="tpu_custom_call" | custom-call | flops 390070272 | bytes 6094848 | tf_op jit(solution)/shard_map/left_terms/pallas_call | solution.py:137
  8.7 2.9 %collective-permute-start.1 = (f32[32,128]{1,0:T(8,128)S(1)}, f32[32,128]{1,0:T(8,128)S(1)}, u32[]{:S(2)}, u32[]{:S(2)}) collective-permute-start(f32[32,128]{1,0:T(8,128)S(1)} %get-tuple-element.25), channel_id=1, source_target_pairs={{0,2},{1,3},{2,0},{3,1},{4,6},{5,7},{6,4},{7,5},{8,10},{9,11},{10,... | collective-permute-start | bytes 49160 | tf_op jit(solution)/shard_map/ppermute | solution.py:52
  11.7 2.0 %collective-permute-done.refs_1_ = f32[32,128]{1,0:T(8,128)S(1)} collective-permute-done((f32[32,128]{1,0:T(8,128)S(1)}, f32[32,128]{1,0:T(8,128)S(1)}, u32[]{:S(2)}, u32[]{:S(2)}) %collective-permute-start) | collective-permute-done | bytes 16416 | tf_op jit(solution)/shard_map/ppermute | solution.py:52
  13.6 2.6 %collective-permute-start.2 = (f32[32,128]{1,0:T(8,128)S(1)}, f32[32,128]{1,0:T(8,128)S(1)}, u32[]{:S(2)}, u32[]{:S(2)}) collective-permute-start(f32[32,128]{1,0:T(8,128)S(1)} %get-tuple-element.26), channel_id=1, source_target_pairs={{0,3},{1,2},{2,1},{3,0},{4,7},{5,6},{6,5},{7,4},{8,11},{9,10},{10,... | collective-permute-start | bytes 49160 | tf_op jit(solution)/shard_map/ppermute | solution.py:52
  17.7 5.0 %collective-permute-start.9 = (f32[32,128]{1,0:T(8,128)S(1)}, f32[32,128]{1,0:T(8,128)S(1)}, u32[]{:S(2)}, u32[]{:S(2)}) collective-permute-start(f32[32,128]{1,0:T(8,128)S(1)} %total.4.refs_0_), channel_id=1, source_target_pairs={{0,28},{4,24},{8,20},{12,16},{16,12},{20,8},{24,4},{28,0},{1,29},{... | collective-permute-start | bytes 49160 | tf_op jit(solution)/shard_map/ppermute | solution.py:52
  23.0 1.5 %collective-permute-done.9.refs_7_ = f32[32,128]{1,0:T(8,128)S(1)} collective-permute-done((f32[32,128]{1,0:T(8,128)S(1)}, f32[32,128]{1,0:T(8,128)S(1)}, u32[]{:S(2)}, u32[]{:S(2)}) %collective-permute-start.9) | collective-permute-done | bytes 16416 | tf_op jit(solution)/shard_map/ppermute | solution.py:52
  24.5 1.9 %collective-permute-start.7 = (f32[32,128]{1,0:T(8,128)S(1)}, f32[32,128]{1,0:T(8,128)S(1)}, u32[]{:S(2)}, u32[]{:S(2)}) collective-permute-start(f32[32,128]{1,0:T(8,128)S(1)} %total.4.refs_0_), channel_id=1, source_target_pairs={{0,20},{4,16},{8,28},{12,24},{16,4},{20,0},{24,12},{28,8},{1,21},{... | collective-permute-start | bytes 49160 | tf_op jit(solution)/shard_map/ppermute | solution.py:52
  26.4 2.2 %collective-permute-done.8.refs_6_ = f32[32,128]{1,0:T(8,128)S(1)} collective-permute-done((f32[32,128]{1,0:T(8,128)S(1)}, f32[32,128]{1,0:T(8,128)S(1)}, u32[]{:S(2)}, u32[]{:S(2)}) %collective-permute-start.8) | collective-permute-done | bytes 16416 | tf_op jit(solution)/shard_map/ppermute | solution.py:52
  28.6 1.5 collective-permute-done.7.refs_5_
  30.1 1.4 collective-permute-start.5
  31.5 1.8 %collective-permute-done.6.refs_4_ = f32[32,128]{1,0:T(8,128)S(1)} collective-permute-done((f32[32,128]{1,0:T(8,128)S(1)}, f32[32,128]{1,0:T(8,128)S(1)}, u32[]{:S(2)}, u32[]{:S(2)}) %collective-permute-start.6) | collective-permute-done | bytes 16416 | tf_op jit(solution)/shard_map/ppermute | solution.py:52
  34.7 1.7 %collective-permute-start.3 = (f32[32,128]{1,0:T(8,128)S(1)}, f32[32,128]{1,0:T(8,128)S(1)}, u32[]{:S(2)}, u32[]{:S(2)}) collective-permute-start(f32[32,128]{1,0:T(8,128)S(1)} %total.4.refs_0_), channel_id=1, source_target_pairs={{0,4},{4,0},{8,12},{12,8},{16,20},{20,16},{24,28},{28,24},{1,5},{5... | collective-permute-start | bytes 49160 | tf_op jit(solution)/shard_map/ppermute | solution.py:52
  37.0 1.5 collective-permute-done.3.refs_1_
  38.5 1.9 %collective-permute-start.11 = (f32[32,128]{1,0:T(8,128)S(1)}, f32[32,128]{1,0:T(8,128)S(1)}, u32[]{:S(2)}, u32[]{:S(2)}) collective-permute-start(f32[32,128]{1,0:T(8,128)S(1)} %total.5.rest_0_), channel_id=1, source_target_pairs={{0,2},{1,3},{2,0},{3,1},{4,6},{5,7},{6,4},{7,5},{8,10},{9,11},{10,... | collective-permute-start | bytes 49160 | tf_op jit(solution)/shard_map/ppermute | solution.py:52
  42.9 6.9 %right_terms.1 = (f32[512,128]{1,0:T(8,128)}, f32[512,128]{1,0:T(8,128)S(1)}) custom-call(s32[1]{0:T(128)} %bitcast.1.me_ref, bf16[512,3968]{1,0:T(8,128)(2,1)} %bitcast.7, f32[128,3968]{1,0:T(8,128)S(1)} %bitcast.16, f32[32,128]{1,0:T(8,128)S(1)} %total.5.rest_0_, f32[32,128]{1,0:T(8,128)S(1)} %collective-permute-done.10.rest_1_, ...), custom_call_target="tpu_custom_call" | custom-call | flops 390070272 | bytes 6094848 | tf_op jit(solution)/shard_map/right_terms/pallas_call | solution.py:230
  51.1 1.4 add_rows.4
  52.5 1.8 %collective-permute-start.34 = (f32[48,3968]{1,0:T(8,128)}, f32[48,3968]{1,0:T(8,128)S(1)}, u32[]{:S(2)}, u32[]{:S(2)}) collective-permute-start(f32[48,3968]{1,0:T(8,128)} %add_rows.4), channel_id=1, source_target_pairs={{0,2},{1,3},{2,0},{3,1},{4,6},{5,7},{6,4},{7,5},{8,10},{9,11},{10,... | collective-permute-start | bytes 2285576 | tf_op jit(solution)/shard_map/ppermute | solution.py:52
  54.3 1.5 add_rows.5
  56.1 1.8 %collective-permute-start.14 = (f32[64,128]{1,0:T(8,128)S(1)}, f32[64,128]{1,0:T(8,128)S(1)}, u32[]{:S(2)}, u32[]{:S(2)}) collective-permute-start(f32[64,128]{1,0:T(8,128)S(1)} %get-tuple-element.32), channel_id=1, source_target_pairs={{0,4},{4,0},{8,12},{12,8},{16,20},{20,16},{24,28},{28,24},{1,5},{5... | collective-permute-start | bytes 98312 | tf_op jit(solution)/shard_map/ppermute | solution.py:52
  57.9 2.2 %collective-permute-done.14.refs_1_ = f32[64,128]{1,0:T(8,128)S(1)} collective-permute-done((f32[64,128]{1,0:T(8,128)S(1)}, f32[64,128]{1,0:T(8,128)S(1)}, u32[]{:S(2)}, u32[]{:S(2)}) %collective-permute-start.14) | collective-permute-done | bytes 32800 | tf_op jit(solution)/shard_map/ppermute | solution.py:52
  60.0 1.5 %collective-permute-start.15 = (f32[64,128]{1,0:T(8,128)S(1)}, f32[64,128]{1,0:T(8,128)S(1)}, u32[]{:S(2)}, u32[]{:S(2)}) collective-permute-start(f32[64,128]{1,0:T(8,128)S(1)} %get-tuple-element.33), channel_id=1, source_target_pairs={{0,8},{4,12},{8,0},{12,4},{16,24},{20,28},{24,16},{28,20},{1,9},{5... | collective-permute-start | bytes 98312 | tf_op jit(solution)/shard_map/ppermute | solution.py:52
  61.6 2.4 %collective-permute-done.15.refs_2_ = f32[64,128]{1,0:T(8,128)S(1)} collective-permute-done((f32[64,128]{1,0:T(8,128)S(1)}, f32[64,128]{1,0:T(8,128)S(1)}, u32[]{:S(2)}, u32[]{:S(2)}) %collective-permute-start.15) | collective-permute-done | bytes 32800 | tf_op jit(solution)/shard_map/ppermute | solution.py:52
  64.0 1.7 %collective-permute-start.16 = (f32[64,128]{1,0:T(8,128)S(1)}, f32[64,128]{1,0:T(8,128)S(1)}, u32[]{:S(2)}, u32[]{:S(2)}) collective-permute-start(f32[64,128]{1,0:T(8,128)S(1)} %get-tuple-element.34), channel_id=1, source_target_pairs={{0,12},{4,8},{8,4},{12,0},{16,28},{20,24},{24,20},{28,16},{1,13},{... | collective-permute-start | bytes 98312 | tf_op jit(solution)/shard_map/ppermute | solution.py:52
  65.6 3.1 %collective-permute-done.16.refs_3_ = f32[64,128]{1,0:T(8,128)S(1)} collective-permute-done((f32[64,128]{1,0:T(8,128)S(1)}, f32[64,128]{1,0:T(8,128)S(1)}, u32[]{:S(2)}, u32[]{:S(2)}) %collective-permute-start.16) | collective-permute-done | bytes 32800 | tf_op jit(solution)/shard_map/ppermute | solution.py:52
  68.8 2.6 %collective-permute-start.17 = (f32[64,128]{1,0:T(8,128)S(1)}, f32[64,128]{1,0:T(8,128)S(1)}, u32[]{:S(2)}, u32[]{:S(2)}) collective-permute-start(f32[64,128]{1,0:T(8,128)S(1)} %get-tuple-element.35), channel_id=1, source_target_pairs={{0,16},{4,20},{8,24},{12,28},{16,0},{20,4},{24,8},{28,12},{1,17},{... | collective-permute-start | bytes 98312 | tf_op jit(solution)/shard_map/ppermute | solution.py:52
  71.3 2.2 %collective-permute-done.17.refs_4_ = f32[64,128]{1,0:T(8,128)S(1)} collective-permute-done((f32[64,128]{1,0:T(8,128)S(1)}, f32[64,128]{1,0:T(8,128)S(1)}, u32[]{:S(2)}, u32[]{:S(2)}) %collective-permute-start.17) | collective-permute-done | bytes 32800 | tf_op jit(solution)/shard_map/ppermute | solution.py:52
  73.6 3.7 %collective-permute-start.18 = (f32[64,128]{1,0:T(8,128)S(1)}, f32[64,128]{1,0:T(8,128)S(1)}, u32[]{:S(2)}, u32[]{:S(2)}) collective-permute-start(f32[64,128]{1,0:T(8,128)S(1)} %get-tuple-element.36), channel_id=1, source_target_pairs={{0,20},{4,16},{8,28},{12,24},{16,4},{20,0},{24,12},{28,8},{1,21},{... | collective-permute-start | bytes 98312 | tf_op jit(solution)/shard_map/ppermute | solution.py:52
  77.3 2.0 %collective-permute-done.18.refs_5_ = f32[64,128]{1,0:T(8,128)S(1)} collective-permute-done((f32[64,128]{1,0:T(8,128)S(1)}, f32[64,128]{1,0:T(8,128)S(1)}, u32[]{:S(2)}, u32[]{:S(2)}) %collective-permute-start.18) | collective-permute-done | bytes 32800 | tf_op jit(solution)/shard_map/ppermute | solution.py:52
  79.3 4.7 %collective-permute-start.19 = (f32[64,128]{1,0:T(8,128)S(1)}, f32[64,128]{1,0:T(8,128)S(1)}, u32[]{:S(2)}, u32[]{:S(2)}) collective-permute-start(f32[64,128]{1,0:T(8,128)S(1)} %get-tuple-element.37), channel_id=1, source_target_pairs={{0,24},{4,28},{8,16},{12,20},{16,8},{20,12},{24,0},{28,4},{1,25},{... | collective-permute-start | bytes 98312 | tf_op jit(solution)/shard_map/ppermute | solution.py:52
  84.0 1.9 %collective-permute-done.19.refs_6_ = f32[64,128]{1,0:T(8,128)S(1)} collective-permute-done((f32[64,128]{1,0:T(8,128)S(1)}, f32[64,128]{1,0:T(8,128)S(1)}, u32[]{:S(2)}, u32[]{:S(2)}) %collective-permute-start.19) | collective-permute-done | bytes 32800 | tf_op jit(solution)/shard_map/ppermute | solution.py:52
  85.9 4.4 %collective-permute-start.20 = (f32[64,128]{1,0:T(8,128)S(1)}, f32[64,128]{1,0:T(8,128)S(1)}, u32[]{:S(2)}, u32[]{:S(2)}) collective-permute-start(f32[64,128]{1,0:T(8,128)S(1)} %get-tuple-element.38), channel_id=1, source_target_pairs={{0,28},{4,24},{8,20},{12,16},{16,12},{20,8},{24,4},{28,0},{1,29},{... | collective-permute-start | bytes 98312 | tf_op jit(solution)/shard_map/ppermute | solution.py:52
  90.3 2.2 %collective-permute-done.20.refs_7_ = f32[64,128]{1,0:T(8,128)S(1)} collective-permute-done((f32[64,128]{1,0:T(8,128)S(1)}, f32[64,128]{1,0:T(8,128)S(1)}, u32[]{:S(2)}, u32[]{:S(2)}) %collective-permute-start.20) | collective-permute-done | bytes 32800 | tf_op jit(solution)/shard_map/ppermute | solution.py:52
  92.6 1.4 collective-permute-start.21
  94.0 2.1 %copy-done.2 = bf16[1,1,512,3968]{3,2,1,0:T(8,128)(2,1)S(1)} copy-done((bf16[1,1,512,3968]{3,2,1,0:T(8,128)(2,1)S(1)}, bf16[1,1,512,3968]{3,2,1,0:T(8,128)(2,1)}, u32[]{:S(2)}) %copy-start.2) | copy-done | bytes 4063256
  96.1 1.8 %add_rows.3 = f32[32,3968]{1,0:T(8,128)} custom-call(s32[1]{0:T(128)S(6)} %xor.4.where_ref, bf16[512,3968]{1,0:T(8,128)(2,1)S(1)} %bitcast.14, f32[32,3968]{1,0:T(8,128)} %collective-permute-done.31.a_ref), custom_call_target="tpu_custom_call" | custom-call | flops 126976 | bytes 1269760 | tf_op jit(solution)/shard_map/add_rows/pallas_call | solution.py:92
  98.6 4.4 %collective-permute-start.28 = (f32[64,128]{1,0:T(8,128)S(1)}, f32[64,128]{1,0:T(8,128)S(1)}, u32[]{:S(2)}, u32[]{:S(2)}) collective-permute-start(f32[64,128]{1,0:T(8,128)S(1)} %total.7.refs_0_), channel_id=1, source_target_pairs={{0,28},{4,24},{8,20},{12,16},{16,12},{20,8},{24,4},{28,0},{1,29},{... | collective-permute-start | bytes 98312 | tf_op jit(solution)/shard_map/ppermute | solution.py:52
  103.1 2.3 %collective-permute-done.28.refs_7_ = f32[64,128]{1,0:T(8,128)S(1)} collective-permute-done((f32[64,128]{1,0:T(8,128)S(1)}, f32[64,128]{1,0:T(8,128)S(1)}, u32[]{:S(2)}, u32[]{:S(2)}) %collective-permute-start.28) | collective-permute-done | bytes 32800 | tf_op jit(solution)/shard_map/ppermute | solution.py:52
  105.4 3.8 %collective-permute-start.27 = (f32[64,128]{1,0:T(8,128)S(1)}, f32[64,128]{1,0:T(8,128)S(1)}, u32[]{:S(2)}, u32[]{:S(2)}) collective-permute-start(f32[64,128]{1,0:T(8,128)S(1)} %total.7.refs_0_), channel_id=1, source_target_pairs={{0,24},{4,28},{8,16},{12,20},{16,8},{20,12},{24,0},{28,4},{1,25},{... | collective-permute-start | bytes 98312 | tf_op jit(solution)/shard_map/ppermute | solution.py:52
  109.2 1.9 %collective-permute-done.27.refs_6_ = f32[64,128]{1,0:T(8,128)S(1)} collective-permute-done((f32[64,128]{1,0:T(8,128)S(1)}, f32[64,128]{1,0:T(8,128)S(1)}, u32[]{:S(2)}, u32[]{:S(2)}) %collective-permute-start.27) | collective-permute-done | bytes 32800 | tf_op jit(solution)/shard_map/ppermute | solution.py:52
  111.1 5.8 %collective-permute-done.26.refs_5_ = f32[64,128]{1,0:T(8,128)S(1)} collective-permute-done((f32[64,128]{1,0:T(8,128)S(1)}, f32[64,128]{1,0:T(8,128)S(1)}, u32[]{:S(2)}, u32[]{:S(2)}) %collective-permute-start.26) | collective-permute-done | bytes 32800 | tf_op jit(solution)/shard_map/ppermute | solution.py:52
  116.9 4.8 %collective-permute-done.25.refs_4_ = f32[64,128]{1,0:T(8,128)S(1)} collective-permute-done((f32[64,128]{1,0:T(8,128)S(1)}, f32[64,128]{1,0:T(8,128)S(1)}, u32[]{:S(2)}, u32[]{:S(2)}) %collective-permute-start.25) | collective-permute-done | bytes 32800 | tf_op jit(solution)/shard_map/ppermute | solution.py:52
  121.7 1.8 %collective-permute-start.24 = (f32[64,128]{1,0:T(8,128)S(1)}, f32[64,128]{1,0:T(8,128)S(1)}, u32[]{:S(2)}, u32[]{:S(2)}) collective-permute-start(f32[64,128]{1,0:T(8,128)S(1)} %total.7.refs_0_), channel_id=1, source_target_pairs={{0,12},{4,8},{8,4},{12,0},{16,28},{20,24},{24,20},{28,16},{1,13},{... | collective-permute-start | bytes 98312 | tf_op jit(solution)/shard_map/ppermute | solution.py:52
  123.6 3.0 %collective-permute-done.24.refs_3_ = f32[64,128]{1,0:T(8,128)S(1)} collective-permute-done((f32[64,128]{1,0:T(8,128)S(1)}, f32[64,128]{1,0:T(8,128)S(1)}, u32[]{:S(2)}, u32[]{:S(2)}) %collective-permute-start.24) | collective-permute-done | bytes 32800 | tf_op jit(solution)/shard_map/ppermute | solution.py:52
  127.9 2.6 %collective-permute-done.23.refs_2_ = f32[64,128]{1,0:T(8,128)S(1)} collective-permute-done((f32[64,128]{1,0:T(8,128)S(1)}, f32[64,128]{1,0:T(8,128)S(1)}, u32[]{:S(2)}, u32[]{:S(2)}) %collective-permute-start.23) | collective-permute-done | bytes 32800 | tf_op jit(solution)/shard_map/ppermute | solution.py:52
  131.6 2.8 %collective-permute-done.22.refs_1_ = f32[64,128]{1,0:T(8,128)S(1)} collective-permute-done((f32[64,128]{1,0:T(8,128)S(1)}, f32[64,128]{1,0:T(8,128)S(1)}, u32[]{:S(2)}, u32[]{:S(2)}) %collective-permute-start.22) | collective-permute-done | bytes 32800 | tf_op jit(solution)/shard_map/ppermute | solution.py:52
  134.5 3.4 %inverse_factor.1 = (f32[32,32]{1,0:T(8,128)S(1)}, f32[32,128]{1,0:T(8,128)S(1)}) custom-call(s32[1]{0:T(128)} %bitcast.1.me_ref, f32[32,128]{1,0:T(8,128)S(1)} %total.5.rest_0_, f32[32,128]{1,0:T(8,128)S(1)} %collective-permute-done.10.rest_1_, f32[32,128]{1,0:T(8,128)S(1)} %collective-permute-done.11.rest_2_, f32[32,128]{1,0:T(8,128)S(1)} %collective-permute-done.12.rest_3_), custom_call_target="tpu_custom_call" | custom-call | flops 3276800 | bytes 32768 | tf_op jit(solution)/shard_map/inverse_factor/pallas_call | solution.py:280
  137.9 2.8 %own_rows.1.p_ref = f32[128,3968]{1,0:T(8,128)S(1)} custom-call(s32[1]{0:T(128)} %bitcast.1.me_ref, bf16[512,3968]{1,0:T(8,128)(2,1)} %bitcast.8, f32[128,3968]{1,0:T(8,128)} %collective-permute-done.30.a_ref, f32[128,3968]{1,0:T(8,128)S(1)} %bitcast.17), custom_call_target="tpu_custom_call" | custom-call | flops 1015808 | bytes 7110656 | tf_op jit(solution)/shard_map/own_rows/pallas_call | solution.py:344
  140.8 8.2 %finish.1 = (f32[128,3968]{1,0:T(8,128)}, f32[128,3968]{1,0:T(8,128)}, f32[32,3968]{1,0:T(8,128)}) custom-call(s32[1]{0:T(128)} %bitcast.core_ref, f32[32,32]{1,0:T(8,128)S(1)} %get-tuple-element.27.inv_ref, f32[32,128]{1,0:T(8,128)S(1)} %get-tuple-element.28.basis_ref, f32[512,128]{1,0:T(8,128)S(1)} %join.1.own_ref, ...), custom_call_target="tpu_custom_call" | custom-call | flops 195035136 | bytes 8126464 | tf_op jit(solution)/shard_map/finish/pallas_call | solution.py:391
  (56 shorter events, 13.5 us)
Async XLA Ops:
  0.6 1.0 copy-start.4
  1.7 6.1 %copy-start = (bf16[1,1,512,3968]{3,2,1,0:T(8,128)(2,1)S(1)}, bf16[1,1,512,3968]{3,2,1,0:T(8,128)(2,1)}, u32[]{:S(2)}) copy-start(bf16[1,1,512,3968]{3,2,1,0:T(8,128)(2,1)} %param.3) | copy-start | bytes 12189700
  7.3 130.6 %collective-permute-start.30 = (f32[128,3968]{1,0:T(8,128)}, f32[128,3968]{1,0:T(8,128)}, u32[]{:S(2)}, u32[]{:S(2)}) collective-permute-start(f32[128,3968]{1,0:T(8,128)} %get-tuple-element.39), channel_id=1, source_target_pairs={{0,1},{1,0},{2,3},{3,2},{4,5},{5,4},{6,7},{7,6},{8,9},{9,8},{10,11... | collective-permute-start | bytes 6094856 | tf_op jit(solution)/shard_map/ppermute | solution.py:52
  7.9 8.4 %copy-start.3 = (f32[1,128,3968]{2,1,0:T(8,128)S(1)}, f32[1,128,3968]{2,1,0:T(8,128)}, u32[]{:S(2)}) copy-start(f32[1,128,3968]{2,1,0:T(8,128)} %param.4) | copy-start | bytes 6094852
  7.9 8.4 %copy-start.5 = (f32[32,3968]{1,0:T(8,128)S(1)}, f32[32,3968]{1,0:T(8,128)}, u32[]{:S(2)}) copy-start(f32[32,3968]{1,0:T(8,128)} %q_ref.3) | copy-start | bytes 1523716
  7.9 43.2 %collective-permute-start.33 = (f32[48,3968]{1,0:T(8,128)S(1)}, f32[48,3968]{1,0:T(8,128)S(1)}, u32[]{:S(2)}, u32[]{:S(2)}) collective-permute-start(f32[48,3968]{1,0:T(8,128)S(1)} %widen_rows.4), channel_id=1, source_target_pairs={{0,1},{1,0},{2,3},{3,2},{4,5},{5,4},{6,7},{7,6},{8,9},{9,8},{10,11... | collective-permute-start | bytes 2285576 | tf_op jit(solution)/shard_map/ppermute | solution.py:52
  8.1 46.2 %collective-permute-start.35 = (f32[48,3968]{1,0:T(8,128)S(1)}, f32[48,3968]{1,0:T(8,128)S(1)}, u32[]{:S(2)}, u32[]{:S(2)}) collective-permute-start(f32[48,3968]{1,0:T(8,128)S(1)} %widen_rows.5), channel_id=1, source_target_pairs={{0,1},{1,0},{2,3},{3,2},{4,5},{5,4},{6,7},{7,6},{8,9},{9,8},{10,11... | collective-permute-start | bytes 2285576 | tf_op jit(solution)/shard_map/ppermute | solution.py:52
  8.6 5.0 %collective-permute-start = (f32[32,128]{1,0:T(8,128)S(1)}, f32[32,128]{1,0:T(8,128)S(1)}, u32[]{:S(2)}, u32[]{:S(2)}) collective-permute-start(f32[32,128]{1,0:T(8,128)S(1)} %get-tuple-element.24), channel_id=1, source_target_pairs={{0,1},{1,0},{2,3},{3,2},{4,5},{5,4},{6,7},{7,6},{8,9},{9,8},{10,11... | collective-permute-start | bytes 49160 | tf_op jit(solution)/shard_map/ppermute | solution.py:52
  8.7 8.7 %collective-permute-start.1 = (f32[32,128]{1,0:T(8,128)S(1)}, f32[32,128]{1,0:T(8,128)S(1)}, u32[]{:S(2)}, u32[]{:S(2)}) collective-permute-start(f32[32,128]{1,0:T(8,128)S(1)} %get-tuple-element.25), channel_id=1, source_target_pairs={{0,2},{1,3},{2,0},{3,1},{4,6},{5,7},{6,4},{7,5},{8,10},{9,11},{10,... | collective-permute-start | bytes 49160 | tf_op jit(solution)/shard_map/ppermute | solution.py:52
  13.6 4.1 %collective-permute-start.2 = (f32[32,128]{1,0:T(8,128)S(1)}, f32[32,128]{1,0:T(8,128)S(1)}, u32[]{:S(2)}, u32[]{:S(2)}) collective-permute-start(f32[32,128]{1,0:T(8,128)S(1)} %get-tuple-element.26), channel_id=1, source_target_pairs={{0,3},{1,2},{2,1},{3,0},{4,7},{5,6},{6,5},{7,4},{8,11},{9,10},{10,... | collective-permute-start | bytes 49160 | tf_op jit(solution)/shard_map/ppermute | solution.py:52
  17.7 6.8 %collective-permute-start.9 = (f32[32,128]{1,0:T(8,128)S(1)}, f32[32,128]{1,0:T(8,128)S(1)}, u32[]{:S(2)}, u32[]{:S(2)}) collective-permute-start(f32[32,128]{1,0:T(8,128)S(1)} %total.4.refs_0_), channel_id=1, source_target_pairs={{0,28},{4,24},{8,20},{12,16},{16,12},{20,8},{24,4},{28,0},{1,29},{... | collective-permute-start | bytes 49160 | tf_op jit(solution)/shard_map/ppermute | solution.py:52
  22.8 5.8 %collective-permute-start.8 = (f32[32,128]{1,0:T(8,128)S(1)}, f32[32,128]{1,0:T(8,128)S(1)}, u32[]{:S(2)}, u32[]{:S(2)}) collective-permute-start(f32[32,128]{1,0:T(8,128)S(1)} %total.4.refs_0_), channel_id=1, source_target_pairs={{0,24},{4,28},{8,16},{12,20},{16,8},{20,12},{24,0},{28,4},{1,25},{... | collective-permute-start | bytes 49160 | tf_op jit(solution)/shard_map/ppermute | solution.py:52
  24.5 5.5 %collective-permute-start.7 = (f32[32,128]{1,0:T(8,128)S(1)}, f32[32,128]{1,0:T(8,128)S(1)}, u32[]{:S(2)}, u32[]{:S(2)}) collective-permute-start(f32[32,128]{1,0:T(8,128)S(1)} %total.4.refs_0_), channel_id=1, source_target_pairs={{0,20},{4,16},{8,28},{12,24},{16,4},{20,0},{24,12},{28,8},{1,21},{... | collective-permute-start | bytes 49160 | tf_op jit(solution)/shard_map/ppermute | solution.py:52
  28.6 4.6 %collective-permute-start.6 = (f32[32,128]{1,0:T(8,128)S(1)}, f32[32,128]{1,0:T(8,128)S(1)}, u32[]{:S(2)}, u32[]{:S(2)}) collective-permute-start(f32[32,128]{1,0:T(8,128)S(1)} %total.4.refs_0_), channel_id=1, source_target_pairs={{0,16},{4,20},{8,24},{12,28},{16,0},{20,4},{24,8},{28,12},{1,17},{... | collective-permute-start | bytes 49160 | tf_op jit(solution)/shard_map/ppermute | solution.py:52
  30.1 4.6 %collective-permute-start.5 = (f32[32,128]{1,0:T(8,128)S(1)}, f32[32,128]{1,0:T(8,128)S(1)}, u32[]{:S(2)}, u32[]{:S(2)}) collective-permute-start(f32[32,128]{1,0:T(8,128)S(1)} %total.4.refs_0_), channel_id=1, source_target_pairs={{0,12},{4,8},{8,4},{12,0},{16,28},{20,24},{24,20},{28,16},{1,13},{... | collective-permute-start | bytes 49160 | tf_op jit(solution)/shard_map/ppermute | solution.py:52
  33.2 3.7 %collective-permute-start.4 = (f32[32,128]{1,0:T(8,128)S(1)}, f32[32,128]{1,0:T(8,128)S(1)}, u32[]{:S(2)}, u32[]{:S(2)}) collective-permute-start(f32[32,128]{1,0:T(8,128)S(1)} %total.4.refs_0_), channel_id=1, source_target_pairs={{0,8},{4,12},{8,0},{12,4},{16,24},{20,28},{24,16},{28,20},{1,9},{5... | collective-permute-start | bytes 49160 | tf_op jit(solution)/shard_map/ppermute | solution.py:52
  34.7 3.7 %collective-permute-start.3 = (f32[32,128]{1,0:T(8,128)S(1)}, f32[32,128]{1,0:T(8,128)S(1)}, u32[]{:S(2)}, u32[]{:S(2)}) collective-permute-start(f32[32,128]{1,0:T(8,128)S(1)} %total.4.refs_0_), channel_id=1, source_target_pairs={{0,4},{4,0},{8,12},{12,8},{16,20},{20,16},{24,28},{28,24},{1,5},{5... | collective-permute-start | bytes 49160 | tf_op jit(solution)/shard_map/ppermute | solution.py:52
  38.4 11.5 %copy-start.1 = (bf16[1,1,512,3968]{3,2,1,0:T(8,128)(2,1)S(1)}, bf16[1,1,512,3968]{3,2,1,0:T(8,128)(2,1)}, u32[]{:S(2)}) copy-start(bf16[1,1,512,3968]{3,2,1,0:T(8,128)(2,1)} %param.3) | copy-start | bytes 12189700
  38.5 3.2 %collective-permute-start.12 = (f32[32,128]{1,0:T(8,128)S(1)}, f32[32,128]{1,0:T(8,128)S(1)}, u32[]{:S(2)}, u32[]{:S(2)}) collective-permute-start(f32[32,128]{1,0:T(8,128)S(1)} %total.5.rest_0_), channel_id=1, source_target_pairs={{0,3},{1,2},{2,1},{3,0},{4,7},{5,6},{6,5},{7,4},{8,11},{9,10},{10,... | collective-permute-start | bytes 49160 | tf_op jit(solution)/shard_map/ppermute | solution.py:52
  38.5 3.8 %collective-permute-start.11 = (f32[32,128]{1,0:T(8,128)S(1)}, f32[32,128]{1,0:T(8,128)S(1)}, u32[]{:S(2)}, u32[]{:S(2)}) collective-permute-start(f32[32,128]{1,0:T(8,128)S(1)} %total.5.rest_0_), channel_id=1, source_target_pairs={{0,2},{1,3},{2,0},{3,1},{4,6},{5,7},{6,4},{7,5},{8,10},{9,11},{10,... | collective-permute-start | bytes 49160 | tf_op jit(solution)/shard_map/ppermute | solution.py:52
  41.7 1.2 collective-permute-start.10
  49.8 6.2 %collective-permute-start.13 = (f32[512,128]{1,0:T(8,128)}, f32[512,128]{1,0:T(8,128)S(1)}, u32[]{:S(2)}, u32[]{:S(2)}) collective-permute-start(f32[512,128]{1,0:T(8,128)} %get-tuple-element.30), channel_id=1, source_target_pairs={{0,1},{1,0},{2,3},{3,2},{4,5},{5,4},{6,7},{7,6},{8,9},{9,8},{10,11... | collective-permute-start | bytes 786440 | tf_op jit(solution)/shard_map/ppermute | solution.py:52
  50.7 43.3 %collective-permute-start.31 = (f32[32,3968]{1,0:T(8,128)}, f32[32,3968]{1,0:T(8,128)}, u32[]{:S(2)}, u32[]{:S(2)}) collective-permute-start(f32[32,3968]{1,0:T(8,128)} %widen_rows.3), channel_id=1, source_target_pairs={{0,1},{1,0},{2,3},{3,2},{4,5},{5,4},{6,7},{7,6},{8,9},{9,8},{10,11... | collective-permute-start | bytes 1523720 | tf_op jit(solution)/shard_map/ppermute | solution.py:52
  52.5 88.2 %collective-permute-start.34 = (f32[48,3968]{1,0:T(8,128)}, f32[48,3968]{1,0:T(8,128)S(1)}, u32[]{:S(2)}, u32[]{:S(2)}) collective-permute-start(f32[48,3968]{1,0:T(8,128)} %add_rows.4), channel_id=1, source_target_pairs={{0,2},{1,3},{2,0},{3,1},{4,6},{5,7},{6,4},{7,5},{8,10},{9,11},{10,... | collective-permute-start | bytes 2285576 | tf_op jit(solution)/shard_map/ppermute | solution.py:52
  55.8 85.0 %collective-permute-start.36 = (f32[48,3968]{1,0:T(8,128)}, f32[48,3968]{1,0:T(8,128)}, u32[]{:S(2)}, u32[]{:S(2)}) collective-permute-start(f32[48,3968]{1,0:T(8,128)} %add_rows.5), channel_id=1, source_target_pairs={{0,2},{1,3},{2,0},{3,1},{4,6},{5,7},{6,4},{7,5},{8,10},{9,11},{10,... | collective-permute-start | bytes 2285576 | tf_op jit(solution)/shard_map/ppermute | solution.py:52
  56.1 4.0 %collective-permute-start.14 = (f32[64,128]{1,0:T(8,128)S(1)}, f32[64,128]{1,0:T(8,128)S(1)}, u32[]{:S(2)}, u32[]{:S(2)}) collective-permute-start(f32[64,128]{1,0:T(8,128)S(1)} %get-tuple-element.32), channel_id=1, source_target_pairs={{0,4},{4,0},{8,12},{12,8},{16,20},{20,16},{24,28},{28,24},{1,5},{5... | collective-permute-start | bytes 98312 | tf_op jit(solution)/shard_map/ppermute | solution.py:52
  60.0 3.9 %collective-permute-start.15 = (f32[64,128]{1,0:T(8,128)S(1)}, f32[64,128]{1,0:T(8,128)S(1)}, u32[]{:S(2)}, u32[]{:S(2)}) collective-permute-start(f32[64,128]{1,0:T(8,128)S(1)} %get-tuple-element.33), channel_id=1, source_target_pairs={{0,8},{4,12},{8,0},{12,4},{16,24},{20,28},{24,16},{28,20},{1,9},{5... | collective-permute-start | bytes 98312 | tf_op jit(solution)/shard_map/ppermute | solution.py:52
  64.0 4.8 %collective-permute-start.16 = (f32[64,128]{1,0:T(8,128)S(1)}, f32[64,128]{1,0:T(8,128)S(1)}, u32[]{:S(2)}, u32[]{:S(2)}) collective-permute-start(f32[64,128]{1,0:T(8,128)S(1)} %get-tuple-element.34), channel_id=1, source_target_pairs={{0,12},{4,8},{8,4},{12,0},{16,28},{20,24},{24,20},{28,16},{1,13},{... | collective-permute-start | bytes 98312 | tf_op jit(solution)/shard_map/ppermute | solution.py:52
  68.8 4.8 %collective-permute-start.17 = (f32[64,128]{1,0:T(8,128)S(1)}, f32[64,128]{1,0:T(8,128)S(1)}, u32[]{:S(2)}, u32[]{:S(2)}) collective-permute-start(f32[64,128]{1,0:T(8,128)S(1)} %get-tuple-element.35), channel_id=1, source_target_pairs={{0,16},{4,20},{8,24},{12,28},{16,0},{20,4},{24,8},{28,12},{1,17},{... | collective-permute-start | bytes 98312 | tf_op jit(solution)/shard_map/ppermute | solution.py:52
  73.6 5.7 %collective-permute-start.18 = (f32[64,128]{1,0:T(8,128)S(1)}, f32[64,128]{1,0:T(8,128)S(1)}, u32[]{:S(2)}, u32[]{:S(2)}) collective-permute-start(f32[64,128]{1,0:T(8,128)S(1)} %get-tuple-element.36), channel_id=1, source_target_pairs={{0,20},{4,16},{8,28},{12,24},{16,4},{20,0},{24,12},{28,8},{1,21},{... | collective-permute-start | bytes 98312 | tf_op jit(solution)/shard_map/ppermute | solution.py:52
  79.3 6.6 %collective-permute-start.19 = (f32[64,128]{1,0:T(8,128)S(1)}, f32[64,128]{1,0:T(8,128)S(1)}, u32[]{:S(2)}, u32[]{:S(2)}) collective-permute-start(f32[64,128]{1,0:T(8,128)S(1)} %get-tuple-element.37), channel_id=1, source_target_pairs={{0,24},{4,28},{8,16},{12,20},{16,8},{20,12},{24,0},{28,4},{1,25},{... | collective-permute-start | bytes 98312 | tf_op jit(solution)/shard_map/ppermute | solution.py:52
  85.9 6.6 %collective-permute-start.20 = (f32[64,128]{1,0:T(8,128)S(1)}, f32[64,128]{1,0:T(8,128)S(1)}, u32[]{:S(2)}, u32[]{:S(2)}) collective-permute-start(f32[64,128]{1,0:T(8,128)S(1)} %get-tuple-element.38), channel_id=1, source_target_pairs={{0,28},{4,24},{8,20},{12,16},{16,12},{20,8},{24,4},{28,0},{1,29},{... | collective-permute-start | bytes 98312 | tf_op jit(solution)/shard_map/ppermute | solution.py:52
  92.6 6.0 %collective-permute-start.21 = (f32[64,128]{1,0:T(8,128)S(1)}, f32[64,128]{1,0:T(8,128)S(1)}, u32[]{:S(2)}, u32[]{:S(2)}) collective-permute-start(f32[64,128]{1,0:T(8,128)S(1)} %total.6.refs_0_), channel_id=1, source_target_pairs={{0,2},{1,3},{2,0},{3,1},{4,6},{5,7},{6,4},{7,5},{8,10},{9,11},{10,... | collective-permute-start | bytes 98312 | tf_op jit(solution)/shard_map/ppermute | solution.py:52
  94.0 2.2 %copy-start.2 = (bf16[1,1,512,3968]{3,2,1,0:T(8,128)(2,1)S(1)}, bf16[1,1,512,3968]{3,2,1,0:T(8,128)(2,1)}, u32[]{:S(2)}) copy-start(bf16[1,1,512,3968]{3,2,1,0:T(8,128)(2,1)} %param.3) | copy-start | bytes 12189700
  97.9 42.8 %collective-permute-start.32 = (f32[32,3968]{1,0:T(8,128)}, f32[32,3968]{1,0:T(8,128)}, u32[]{:S(2)}, u32[]{:S(2)}) collective-permute-start(f32[32,3968]{1,0:T(8,128)} %add_rows.3), channel_id=1, source_target_pairs={{0,2},{1,3},{2,0},{3,1},{4,6},{5,7},{6,4},{7,5},{8,10},{9,11},{10,... | collective-permute-start | bytes 1523720 | tf_op jit(solution)/shard_map/ppermute | solution.py:52
  98.6 6.8 %collective-permute-start.28 = (f32[64,128]{1,0:T(8,128)S(1)}, f32[64,128]{1,0:T(8,128)S(1)}, u32[]{:S(2)}, u32[]{:S(2)}) collective-permute-start(f32[64,128]{1,0:T(8,128)S(1)} %total.7.refs_0_), channel_id=1, source_target_pairs={{0,28},{4,24},{8,20},{12,16},{16,12},{20,8},{24,4},{28,0},{1,29},{... | collective-permute-start | bytes 98312 | tf_op jit(solution)/shard_map/ppermute | solution.py:52
  105.4 5.7 %collective-permute-start.27 = (f32[64,128]{1,0:T(8,128)S(1)}, f32[64,128]{1,0:T(8,128)S(1)}, u32[]{:S(2)}, u32[]{:S(2)}) collective-permute-start(f32[64,128]{1,0:T(8,128)S(1)} %total.7.refs_0_), channel_id=1, source_target_pairs={{0,24},{4,28},{8,16},{12,20},{16,8},{20,12},{24,0},{28,4},{1,25},{... | collective-permute-start | bytes 98312 | tf_op jit(solution)/shard_map/ppermute | solution.py:52
  111.1 5.8 %collective-permute-start.26 = (f32[64,128]{1,0:T(8,128)S(1)}, f32[64,128]{1,0:T(8,128)S(1)}, u32[]{:S(2)}, u32[]{:S(2)}) collective-permute-start(f32[64,128]{1,0:T(8,128)S(1)} %total.7.refs_0_), channel_id=1, source_target_pairs={{0,20},{4,16},{8,28},{12,24},{16,4},{20,0},{24,12},{28,8},{1,21},{... | collective-permute-start | bytes 98312 | tf_op jit(solution)/shard_map/ppermute | solution.py:52
  116.9 4.8 %collective-permute-start.25 = (f32[64,128]{1,0:T(8,128)S(1)}, f32[64,128]{1,0:T(8,128)S(1)}, u32[]{:S(2)}, u32[]{:S(2)}) collective-permute-start(f32[64,128]{1,0:T(8,128)S(1)} %total.7.refs_0_), channel_id=1, source_target_pairs={{0,16},{4,20},{8,24},{12,28},{16,0},{20,4},{24,8},{28,12},{1,17},{... | collective-permute-start | bytes 98312 | tf_op jit(solution)/shard_map/ppermute | solution.py:52
  121.7 4.8 %collective-permute-start.24 = (f32[64,128]{1,0:T(8,128)S(1)}, f32[64,128]{1,0:T(8,128)S(1)}, u32[]{:S(2)}, u32[]{:S(2)}) collective-permute-start(f32[64,128]{1,0:T(8,128)S(1)} %total.7.refs_0_), channel_id=1, source_target_pairs={{0,12},{4,8},{8,4},{12,0},{16,28},{20,24},{24,20},{28,16},{1,13},{... | collective-permute-start | bytes 98312 | tf_op jit(solution)/shard_map/ppermute | solution.py:52
  126.6 3.9 %collective-permute-start.23 = (f32[64,128]{1,0:T(8,128)S(1)}, f32[64,128]{1,0:T(8,128)S(1)}, u32[]{:S(2)}, u32[]{:S(2)}) collective-permute-start(f32[64,128]{1,0:T(8,128)S(1)} %total.7.refs_0_), channel_id=1, source_target_pairs={{0,8},{4,12},{8,0},{12,4},{16,24},{20,28},{24,16},{28,20},{1,9},{5... | collective-permute-start | bytes 98312 | tf_op jit(solution)/shard_map/ppermute | solution.py:52
  130.5 3.9 %collective-permute-start.22 = (f32[64,128]{1,0:T(8,128)S(1)}, f32[64,128]{1,0:T(8,128)S(1)}, u32[]{:S(2)}, u32[]{:S(2)}) collective-permute-start(f32[64,128]{1,0:T(8,128)S(1)} %total.7.refs_0_), channel_id=1, source_target_pairs={{0,4},{4,0},{8,12},{12,8},{16,20},{20,16},{24,28},{28,24},{1,5},{5... | collective-permute-start | bytes 98312 | tf_op jit(solution)/shard_map/ppermute | solution.py:52
  134.4 6.3 %collective-permute-start.29 = (f32[512,128]{1,0:T(8,128)S(1)}, f32[512,128]{1,0:T(8,128)S(1)}, u32[]{:S(2)}, u32[]{:S(2)}) collective-permute-start(f32[512,128]{1,0:T(8,128)S(1)} %join.1.own_ref), channel_id=1, source_target_pairs={{0,1},{1,0},{2,3},{3,2},{4,5},{5,4},{6,7},{7,6},{8,9},{9,8},{10,11... | collective-permute-start | bytes 786440 | tf_op jit(solution)/shard_map/ppermute | solution.py:52

commit v2 on v0

v2 whole, which is shorter than its diff:
```python
import jax
import jax.numpy as jnp
from jax import lax
from jax.experimental import pallas as pl
from jax.experimental.pallas import tpu as pltpu
from jax.sharding import Mesh, PartitionSpec as P

F32 = jnp.float32
BF16 = jnp.bfloat16
LANES = 128
WIDE = 512
VMEM_LIMIT = 24 * 1024 * 1024


def pieces(x):
    high = x.astype(BF16)
    rest = x - high.astype(F32)
    mid = rest.astype(BF16)
    low = (rest - mid.astype(F32)).astype(BF16)
    return jnp.concatenate([high, mid, low], axis=0)


def fold(x, rank):
    return (x[2 * rank :] + x[rank : 2 * rank]) + x[:rank]


def dot(a, b, contract, precision=None):
    return lax.dot_general(
        a, b, (contract, ((), ())), precision=precision, preferred_element_type=F32
    )


def six(x, axis, left):
    high = x.astype(BF16)
    rest = x - high.astype(F32)
    mid = rest.astype(BF16)
    low = (rest - mid.astype(F32)).astype(BF16)
    order = [high, high, mid, high, low, mid] if left else [high, mid, high, low, high, mid]
    return jnp.concatenate(order, axis=axis)


def params(limit=VMEM_LIMIT):
    return pltpu.CompilerParams(vmem_limit_bytes=limit)


NO_COST = pl.CostEstimate(flops=0, bytes_accessed=0, transcendentals=0)


def partner(x, axis, d):
    return lax.ppermute(x, axis, [(i, i ^ d) for i in range(lax.axis_size(axis))])


def whole(shape):
    return pl.BlockSpec(shape, lambda *_: (0,) * len(shape))


ANYWHERE = pl.BlockSpec(memory_space=pl.ANY)
VMEM = pl.BlockSpec(memory_space=pltpu.VMEM)
SMEM = pl.BlockSpec(memory_space=pltpu.SMEM)
HBM = pl.BlockSpec(memory_space=pltpu.HBM)


def exchange(parts, axes):
    return lax.all_to_all(parts, axes, split_axis=0, concat_axis=0, tiled=True)


def tree(values):
    values = list(values)
    while len(values) > 1:
        values = [sum(values[i + 1 : i + 2], values[i]) for i in range(0, len(values), 2)]
    return values[0]


def total(values, after=(), repeat=None):
    n = len(values)
    shape = values[0].shape

    def kernel(*refs):
        value = tree([r[...] for r in refs[:n]])
        if repeat is None:
            refs[-1][...] = value
        else:
            for k in range(repeat):
                refs[-1][k] = value

    return pl.pallas_call(
        kernel,
        out_shape=jax.ShapeDtypeStruct(shape if repeat is None else (repeat, *shape), F32),
        in_specs=[VMEM] * n + [ANYWHERE] * len(after),
        out_specs=VMEM,
        compiler_params=params(),
        cost_estimate=NO_COST,
        name="total",
    )(*values, *after)


def sum_parts(parts, after=()):
    n = parts.shape[0]

    def kernel(p_ref, *rest):
        rest[-1][...] = tree([p_ref[k] for k in range(n)])

    return pl.pallas_call(
        kernel,
        out_shape=jax.ShapeDtypeStruct(parts.shape[1:], F32),
        in_specs=[VMEM] + [ANYWHERE] * len(after),
        out_specs=VMEM,
        compiler_params=params(),
        cost_estimate=NO_COST,
        name="sum_parts",
    )(parts, *after)


def passed_on(value, after):
    def kernel(*refs):
        pass

    return pl.pallas_call(
        kernel,
        out_shape=jax.ShapeDtypeStruct(value.shape, value.dtype),
        in_specs=[ANYWHERE] * (1 + len(after)),
        out_specs=ANYWHERE,
        input_output_aliases={0: 0},
        compiler_params=params(),
        cost_estimate=NO_COST,
        name="passed_on",
    )(value, *after)


def join(me_ref, own_ref, other_ref, f_all):
    n_shard, rank, _ = f_all.shape
    half = n_shard // 2
    core = me_ref[0] & 1
    for k in range(half):
        f_all[2 * k + core] = own_ref[k * rank : (k + 1) * rank]
        f_all[2 * k + 1 - core] = other_ref[k * rank : (k + 1) * rank]


def spans(size, step):
    return [(at, min(step, size - at)) for at in range(0, size, step)]


def started(source, target, sem):
    copy = pltpu.make_async_copy(source, target, sem)
    copy.start()
    return copy


def add_rows(where, grads, arrived, cuts, after=()):
    block, cols = arrived.shape

    def kernel(where_ref, g_ref, a_ref, *rest):
        outs = rest[len(after) :]
        first = pl.multiple_of(where_ref[0] * block, block)
        for (at, n), out in zip(cuts, outs):
            rows = pl.ds(pl.multiple_of(first + at, 16), n)
            out[...] = g_ref[rows, :].astype(F32) + a_ref[at : at + n, :]

    return pl.pallas_call(
        kernel,
        out_shape=[jax.ShapeDtypeStruct((count, cols), F32) for _, count in cuts],
        in_specs=[SMEM, VMEM, VMEM] + [ANYWHERE] * len(after),
        out_specs=[VMEM] * len(cuts),
        compiler_params=params(),
        cost_estimate=NO_COST,
        name="add_rows",
    )(where, grads, arrived, *after)


def left_terms(me, grads, q_factor, n_shard):
    rows, cols = grads.shape
    block = rows // n_shard
    rank = q_factor.shape[0]
    half = n_shard // 2
    parts = spans(cols, 2 * WIDE)
    out = jax.ShapeDtypeStruct((half * rank, block), F32)

    def kernel(me_ref, g_ref, q_ref, send_ref, keep_ref, qt_ref, *rest):
        wide_refs, acc = rest[:half], rest[half]
        mm = ((1,), (0,))
        for k, (at, n) in enumerate(parts):
            c = slice(at, at + n)
            q3 = pieces(q_ref[:, c]).astype(F32)
            padded = jnp.concatenate([q3, jnp.zeros((LANES - 3 * rank, n), F32)], axis=0)
            q = padded.T.astype(BF16)
            qt_ref[c, :] = q
            value = dot(g_ref[:, c], q, mm)
            acc[...] = value if k == 0 else acc[...] + value
            for d, wide_ref in enumerate(wide_refs):
                first = pl.multiple_of((me_ref[0] ^ (2 * d + 1)) * block, block)
                wide_ref[:, c] = g_ref[pl.ds(first, block), c].astype(F32)
        core = me_ref[0] & 1
        for k in range(half):
            for ref, owner in ((send_ref, 1 - core), (keep_ref, core)):
                first = pl.multiple_of((2 * k + owner) * block, block)
                term = acc[pl.ds(first, block), :].T
                ref[k * rank : (k + 1) * rank, :] = fold(term[: 3 * rank], rank)

    return pl.pallas_call(
        kernel,
        out_shape=[out, out, jax.ShapeDtypeStruct((cols, LANES), BF16)]
        + [jax.ShapeDtypeStruct((block, cols), F32)] * half,
        in_specs=[SMEM, VMEM, VMEM],
        out_specs=[VMEM] * (3 + half),
        scratch_shapes=[pltpu.VMEM((rows, LANES), F32)],
        compiler_params=params(),
        cost_estimate=NO_COST,
        name="left_terms",
    )(me, grads, q_factor)


def error_term(me, error, q_columns, shape, rank):
    block, cols = error.shape
    parts = spans(cols, 2 * WIDE)

    def kernel(me_ref, e_ref, q_ref, out_ref):
        mm = ((1,), (0,))
        value = jnp.zeros((block, LANES), F32)
        for at, n in parts:
            e = e_ref[:, at : at + n]
            q = q_ref[at : at + n, :]
            high = e.astype(BF16)
            mid = (e - high.astype(F32)).astype(BF16)
            value = value + (dot(high, q, mm) + dot(mid, q, mm))
        term = fold(value.T[: 3 * rank], rank)
        for k in range(shape[0] // rank):
            mine = me_ref[0] // 2 == k
            out_ref[k * rank : (k + 1) * rank, :] = jnp.where(mine, term, 0.0)

    return pl.pallas_call(
        kernel,
        out_shape=jax.ShapeDtypeStruct(shape, F32),
        in_specs=[SMEM, VMEM, VMEM],
        out_specs=VMEM,
        compiler_params=params(),
        cost_estimate=NO_COST,
        name="error_term",
    )(me, error, q_columns)


def right_terms(me, grads, error, halves, rank, n_shard, after):
    rows, cols = grads.shape
    block = rows // n_shard
    per = WIDE // LANES
    parts = spans(cols, WIDE)
    n_half = -(-len(parts) // 2)
    out = jax.ShapeDtypeStruct((n_half * per * rank, LANES), F32)

    def kernel(me_ref, g_ref, e_ref, own_ref, other_ref, *rest):
        send_ref, keep_ref, f_all = rest[len(after) :]
        join(me_ref, own_ref, other_ref, f_all)
        f3 = pieces(jnp.concatenate([f_all[j] for j in range(n_shard)], axis=1))
        own = pieces(f_all[me_ref[0]])
        f_own = jnp.concatenate([own, own], axis=1)
        core = me_ref[0] & 1
        mm = ((1,), (0,))
        for k, (at, n) in enumerate(parts):
            c = slice(at, at + n)
            e = e_ref[:, c]
            high = e.astype(BF16)
            mid = (e - high.astype(F32)).astype(BF16)
            value = dot(f3, g_ref[:, c], mm)
            value += dot(f_own, jnp.concatenate([high, mid], axis=0), mm)
            value = fold(value, rank)
            if n < WIDE:
                value = jnp.concatenate([value, jnp.zeros((rank, WIDE - n), F32)], axis=1)
            stacked = jnp.concatenate(
                [value[:, b * LANES : (b + 1) * LANES] for b in range(per)], axis=0
            )
            at_rows = slice((k % n_half) * per * rank, (k % n_half + 1) * per * rank)

            @pl.when(core == k // n_half)
            def _(stacked=stacked, at_rows=at_rows):
                keep_ref[at_rows, :] = stacked

            @pl.when(core != k // n_half)
            def _(stacked=stacked, at_rows=at_rows):
                send_ref[at_rows, :] = stacked

    return pl.pallas_call(
        kernel,
        out_shape=[out, out],
        in_specs=[SMEM, VMEM, VMEM, VMEM, VMEM] + [ANYWHERE] * len(after),
        out_specs=[VMEM, VMEM],
        scratch_shapes=[pltpu.VMEM((n_shard, rank, block), F32)],
        compiler_params=params(),
        cost_estimate=NO_COST,
        name="right_terms",
    )(me, grads, error, *halves, *after)


def finish(core, both, q_own, q_other, partial, arrived):
    rows, cols = partial.shape
    rank = both.shape[0] - rows
    per = WIDE // LANES
    parts = spans(cols, WIDE)
    row_parts = spans(rows, 32)
    n_half = q_own.shape[0] // (per * rank)
    counts = [a.shape[0] for a in arrived]
    n_arrived = len(arrived)

    def kernel(core_ref, both_ref, own_ref, other_ref, p_ref, *rest):
        a_refs = rest[:n_arrived]
        approx_ref, error_ref, q_ref, o_buf, n_buf, q_buf, sems = rest[n_arrived:]
        out = []
        left = both_ref[...]
        for k, (at, n) in enumerate(parts):
            c = slice(at, at + n)
            at_rows = slice((k % n_half) * per * rank, (k % n_half + 1) * per * rank)
            mine = core_ref[0] == k // n_half
            stacked = jnp.where(mine, own_ref[at_rows, :], other_ref[at_rows, :])
            q_sum = jnp.concatenate(
                [stacked[b * rank : (b + 1) * rank] for b in range(n // LANES)], axis=1
            )
            value = dot(left, six(q_sum, 0, False), ((1,), (0,)))
            q_buf[:, c] = value[:rank]
            o_buf[:, c] = value[rank:]
        out.append(started(q_buf, q_ref, sems.at[0, 0]))
        for k, (at, n) in enumerate(row_parts):
            r = pl.ds(at, n)
            out.append(started(o_buf.at[r, :], approx_ref.at[r, :], sems.at[1, k]))
        first = 0
        for count, a_ref in zip(counts, a_refs):
            for at, n in spans(count, 16):
                r = slice(first + at, first + at + n)
                n_buf[r, :] = (p_ref[r, :] + a_ref[at : at + n, :]) - o_buf[r, :]
                rows_out = pl.ds(first + at, n)
                k = (first + at) // 16
                out.append(started(n_buf.at[rows_out, :], error_ref.at[rows_out, :], sems.at[2, k]))
            first += count
        for copy in out:
            copy.wait()

    return pl.pallas_call(
        kernel,
        out_shape=[
            jax.ShapeDtypeStruct((rows, cols), F32),
            jax.ShapeDtypeStruct((rows, cols), F32),
            jax.ShapeDtypeStruct((rank, cols), F32),
        ],
        in_specs=[SMEM] + [VMEM] * (4 + n_arrived),
        out_specs=[ANYWHERE] * 3,
        scratch_shapes=[pltpu.VMEM((rows, cols), F32)] * 2
        + [
            pltpu.VMEM((rank, cols), F32),
            pltpu.SemaphoreType.DMA((3, -(-rows // 16))),
        ],
        compiler_params=params(),
        cost_estimate=NO_COST,
        name="finish",
    )(core, both, q_own, q_other, partial, *arrived)


def inverse_factor(me, halves, rank, n_rep, n_shard, after):
    block = halves[0].shape[1]

    def kernel(me_ref, own_ref, other_ref, *rest):
        both_ref, f_all = rest[-2:]
        join(me_ref, own_ref, other_ref, f_all)
        f = jnp.concatenate([f_all[j] for j in range(n_shard)], axis=1)
        gram = dot(f, f, ((1,), (1,)), lax.Precision.HIGHEST)
        row = lax.broadcasted_iota(jnp.int32, (rank, 2 * rank), 0)
        col = lax.broadcasted_iota(jnp.int32, (rank, 2 * rank), 1)
        unit = jnp.where(col == row + rank, 1.0, 0.0).astype(F32)
        w = jnp.concatenate([gram, jnp.zeros_like(gram)], axis=1) + unit
        for k in range(rank):
            column = w[:, k : k + 1] * (1.0 / w[k : k + 1, k : k + 1])
            w = jnp.where(row > k, w - column * w[k : k + 1, :], w)
        pivots = jnp.sum(jnp.where(row == col, w, 0.0), axis=1, keepdims=True)
        w = w * (1.0 / jnp.sqrt(pivots))
        inverse = w[:, rank:]
        basis = dot(inverse, f_all[me_ref[0]], ((1,), (0,)), lax.Precision.HIGHEST)
        to_approx = dot(basis.T, inverse, ((1,), (0,)), lax.Precision.HIGHEST)
        both = jnp.concatenate([inverse, to_approx], axis=0) * (1.0 / n_rep)
        both_ref[...] = six(both, 1, True)

    return pl.pallas_call(
        kernel,
        out_shape=jax.ShapeDtypeStruct((rank + block, 6 * rank), BF16),
        in_specs=[SMEM, VMEM, VMEM] + [ANYWHERE] * len(after),
        out_specs=VMEM,
        scratch_shapes=[pltpu.VMEM((n_shard, rank, block), F32)],
        compiler_params=params(),
        cost_estimate=NO_COST,
        name="inverse_factor",
    )(me, *halves, *after)


def group_sum(value, axes, first, bits, after=()):
    moved = [partner(value, axes, d << first) for d in range(1, 1 << bits)]
    return total([value, *moved], after)


def pair_sum(value, axes, bit, after=()):
    return total([value, partner(value, axes, 1 << bit)], after)


def body(grads, error, q_factor):
    n_rep, n_y = lax.axis_size("rep"), lax.axis_size("y")
    n_shard = 2 * n_y
    grads, error = grads[0, 0], error[0]
    rows, cols = grads.shape
    block = rows // n_shard
    rank = q_factor.shape[0]
    core = lax.axis_index("core").astype(jnp.int32)
    here = 2 * lax.axis_index("y").astype(jnp.int32) + core
    me, core = here.reshape(1), core.reshape(1)
    chips = ("rep", "y")
    n_bits = (n_rep * n_y).bit_length() - 1
    distances = range(1, n_y)
    cuts = [(0, 80), (80, block - 80)]

    send, keep, q_columns, own_wide, *wide = left_terms(me, grads, q_factor, n_shard)
    from_other = partner(send, "core", 1)
    half = total([keep, from_other, error_term(me, error, q_columns, keep.shape, rank)])
    sums = [
        add_rows(me ^ (2 * d), grads, partner(passed_on(w, [half]), "core", 1), cuts)
        for d, w in zip(distances, wide)
    ]

    def over_y(k, after=None):
        values = [value[k] for value in sums]
        if after is not None:
            values = [passed_on(value, after) for value in values]
        moved = [partner(value, "y", d) for d, value in zip(distances, values)]
        return values, moved[0] if n_y == 2 else sum(moved)

    half = pair_sum(half, chips, 0)
    crossing, first_part = over_y(0, [half])
    from_core = partner(passed_on(own_wide, [half]), "core", 1)
    half = pair_sum(half, chips, 1, [value[0] for value in sums])
    half = group_sum(half, chips, 2, n_bits - 2, crossing)
    halves = [half, partner(half, "core", 1)]

    send, keep = right_terms(me, grads, error, halves, rank, n_shard, [from_core])
    both = inverse_factor(me, halves, rank, n_rep, n_shard, [send])
    own_half = total([keep, partner(send, "core", 1)], [both])
    parts = exchange(own_half.reshape(n_rep, -1, LANES), "rep")
    piece = sum_parts(parts, [first_part])
    values, second_part = over_y(1, [piece])
    piece = [piece] + [partner(piece, "y", d) for d in distances]
    pieces_out = total(piece, values, n_rep)
    own_terms = lax.dynamic_slice(grads, (here * block, 0), (block, cols)).astype(F32)
    partial = (own_terms + from_core) + error
    q_own = exchange(pieces_out, "rep").reshape(own_half.shape)
    q_own = passed_on(q_own, [partial])
    q_other = partner(q_own, "core", 1)

    arrived = [first_part, second_part]
    approx, new_error, q_next = finish(core, both, q_own, q_other, partial, arrived)
    return approx, new_error[None], q_next


def solution(mesh):
    n_rep, n_shard = mesh.devices.shape
    mesh = Mesh(mesh.devices.reshape(n_rep, n_shard // 2, 2), ("rep", "y", "core"))
    shard = ("y", "core")
    in_specs = (P("rep", shard, None, None), P("rep", shard, None), P())
    out_specs = (P(shard, None), P("rep", shard, None), P())
    return jax.shard_map(body, mesh=mesh, in_specs=in_specs, out_specs=out_specs, check_vma=False)
```

time: 283 us -> 71.1 us (0.25)
  waiting for transfers between devices: 197 us -> 17.7 us
  blocking collectives: 47.3 us -> 13.5 us
  starting transfers between devices: 0.08 us -> 18.6 us
  Pallas kernels: 0 us -> 14.1 us
  between operations: 14.1 us -> 0.76 us
  other arithmetic: 15.6 us -> 2.74 us
  matrix products: 9.32 us -> 0 us
  local copies, waits for them, and re-layouts: 0.29 us -> 3.2 us
    psum x1 -> x0, waiting for transfers between devices: 124 us -> none  [body(): q_total_sum = lax.psum(q_term, ('rep', 'shard'))]
    reduce_scatter x1 -> x0, waiting for transfers between devices: 73 us -> none  [body(): lax.psum_scatter(local_grad, 'shard', scatter_dimension=0, tiled=True)]
    psum x2 -> x0, blocking collectives: 47.3 us -> none  [the longest x1 37.1 us: body(): own_factor = lax.psum(factor_term, 'rep')]
    ppermute x0 -> x14, starting transfers between devices: none -> 14.5 us  [partner(): lax.ppermute(x, axis, [(i, i ^ d) for i in range(lax.axis_size(axis))])]
    pallas_call x0 -> x18, Pallas kernels: none -> 14.1 us  [the longest x1 4.16 us: finish(): pl.pallas_call(kernel, out_shape=[jax.ShapeDtypeStruct((rows, cols), F32)...]
    all_to_all x0 -> x1, blocking collectives: none -> 13.5 us  [exchange(): return lax.all_to_all(parts, axes, split_axis=0, concat_axis=0, tiled=True)]
    ppermute x0 -> x14, waiting for transfers between devices: none -> 12.2 us  [partner(): lax.ppermute(x, axis, [(i, i ^ d) for i in range(lax.axis_size(axis))])]
    dot_general x4 -> x0, matrix products: 9.11 us -> none  [the longest x1 3.61 us: body(): jnp.dot(basis_rows, merged, precision=lax.Precision.HIGHEST, preferred_el...]
  transfers between devices with their start and end apart: 2 -> 15, of which waited for: 2 -> 9; matrix products, arithmetic and copies ran while one was open for 0% -> 4% of each run, Pallas kernels for 0% -> 12%
where the time goes in v2:
time: 71.1 us; the launch traced here: 70.7 us
  starting transfers between devices  18.6 us (26%)
  waiting for transfers between devices  17.7 us (25%)
  Pallas kernels  14.1 us (20%)
  blocking collectives  13.5 us (19%)
  local copies, waits for them, and re-layouts  3.2 us (5%)
  other arithmetic  2.74 us (4%)
  between operations  0.76 us (1%)
    ppermute x14, starting transfers between devices, partner(): lax.ppermute(x, axis, [(i, i ^ d) for i in range(lax.axis_size(axis))])  14.5 us
    all_to_all x1, blocking collectives, exchange(): return lax.all_to_all(parts, axes, split_axis=0, concat_axis=0, tiled=True)  13.5 us
    ppermute x14, waiting for transfers between devices, partner(): lax.ppermute(x, axis, [(i, i ^ d) for i in range(lax.axis_size(axis))])  12.2 us
    all_to_all x1, waiting for transfers between devices, exchange(): return lax.all_to_all(parts, axes, split_axis=0, concat_axis=0, tiled=True)  5.58 us
    pallas_call x1, Pallas kernels, finish(): pl.pallas_call(kernel, out_shape=[jax.ShapeDtypeStruct((rows, cols), F32)...  4.16 us
    all_to_all x1, starting transfers between devices, exchange(): return lax.all_to_all(parts, axes, split_axis=0, concat_axis=0, tiled=True)  4.15 us
    pallas_call x1, Pallas kernels, inverse_factor(): pl.pallas_call(kernel, out_shape=jax.ShapeDtypeStruct((rank + block, 6 *...  3.52 us
    unnamed x10, local copies, waits for them, and re-layouts  3.2 us
  transfers between devices with their start and end apart: 15, of which 9 were waited for; matrix products, arithmetic and copies ran while one was open for 4% of the time, Pallas kernels for 12%

profile of v2, /device:TPU:0, one launch (start us, length us, event | category | flops | bytes accessed | tf_op | source)
XLA Modules:
  0.0 70.7 jit_solution(3982335574361324568)
XLA Ops:
  0.6 0.0 copy-start
  0.6 2.1 %copy-done = bf16[1,1,512,3968]{3,2,1,0:T(8,128)(2,1)S(1)} copy-done((bf16[1,1,512,3968]{3,2,1,0:T(8,128)(2,1)S(1)}, bf16[1,1,512,3968]{3,2,1,0:T(8,128)(2,1)}, u32[]{:S(2)}) %copy-start) | copy-done | bytes 4063256
  2.8 0.0 copy-start.4
  2.8 1.0 %copy-done.4 = f32[32,3968]{1,0:T(8,128)S(1)} copy-done((f32[32,3968]{1,0:T(8,128)S(1)}, f32[32,3968]{1,0:T(8,128)}, u32[]{:S(2)}) %copy-start.4) | copy-done | bytes 507928
  3.8 0.0 copy-start.2
  3.8 1.6 %left_terms.1 = (f32[64,128]{1,0:T(8,128)S(1)}, f32[64,128]{1,0:T(8,128)S(1)}, bf16[3968,128]{1,0:T(8,128)(2,1)S(1)}, f32[128,3968]{1,0:T(8,128)S(1)}, f32[128,3968]{1,0:T(8,128)S(1)}) custom-call(s32[1]{0:T(128)} %bitcast.1.me_ref, bf16[512,3968]{1,0:T(8,128)(2,1)S(1)} %bitcast.11, f32[32,3968]{1,0:T(8,128)S(1)} %copy-done.4), custom_call_target="tpu_custom_call" | custom-call | tf_op jit(solution)/shard_map/left_terms/pallas_call | solution.py:199
  5.5 0.5 collective-permute-start
  6.0 0.0 copy-done.2
  6.0 0.8 %error_term.1.refs_2_ = f32[64,128]{1,0:T(8,128)S(1)} custom-call(s32[1]{0:T(128)} %bitcast.1.me_ref, f32[128,3968]{1,0:T(8,128)S(1)} %bitcast.14, bf16[3968,128]{1,0:T(8,128)(2,1)S(1)} %get-tuple-element.17.q_ref), custom_call_target="tpu_custom_call" | custom-call | tf_op jit(solution)/shard_map/error_term/pallas_call | solution.py:230
  6.8 0.1 collective-permute-done.refs_1_
  6.9 0.4 collective-permute-start.3
  7.3 2.7 %collective-permute-start.1 = (f32[64,128]{1,0:T(8,128)S(1)}, f32[64,128]{1,0:T(8,128)S(1)}, u32[]{:S(2)}, u32[]{:S(2)}) collective-permute-start(f32[64,128]{1,0:T(8,128)S(1)} %total.6.refs_0_.refs_1_), channel_id=1, source_target_pairs={{0,2},{2,0},{4,6},{6,4},{8,10},{10,8},{12,14},{14,12},{16,18},{18,... | collective-permute-start | bytes 98312 | tf_op jit(solution)/shard_map/ppermute | solution.py:50
  10.0 1.9 %collective-permute-done.1.refs_1_ = f32[64,128]{1,0:T(8,128)S(1)} collective-permute-done((f32[64,128]{1,0:T(8,128)S(1)}, f32[64,128]{1,0:T(8,128)S(1)}, u32[]{:S(2)}, u32[]{:S(2)}) %collective-permute-start.1) | collective-permute-done | bytes 32800 | tf_op jit(solution)/shard_map/ppermute | solution.py:50
  11.9 0.1 collective-permute-start.8
  12.0 2.1 %collective-permute-start.2 = (f32[64,128]{1,0:T(8,128)S(1)}, f32[64,128]{1,0:T(8,128)S(1)}, u32[]{:S(2)}, u32[]{:S(2)}) collective-permute-start(f32[64,128]{1,0:T(8,128)S(1)} %total.7.refs_0_.refs_1_), channel_id=1, source_target_pairs={{0,4},{2,6},{4,0},{6,2},{8,12},{10,14},{12,8},{14,10},{16,20},{18,... | collective-permute-start | bytes 98312 | tf_op jit(solution)/shard_map/ppermute | solution.py:50
  14.0 0.0 collective-permute-done.3.a_ref
  14.0 0.0 copy-done.1
  14.0 1.1 %add_rows.1 = (f32[80,3968]{1,0:T(8,128)S(1)}, f32[48,3968]{1,0:T(8,128)}) custom-call(s32[1]{0:T(128)S(6)} %xor.3.where_ref, bf16[512,3968]{1,0:T(8,128)(2,1)S(1)} %bitcast.12, f32[128,3968]{1,0:T(8,128)S(1)} %collective-permute-done.3.a_ref), custom_call_target="tpu_custom_call" | custom-call | tf_op jit(solution)/shard_map/add_rows/pallas_call | solution.py:159
  15.1 0.9 %collective-permute-done.2.refs_1_ = f32[64,128]{1,0:T(8,128)S(1)} collective-permute-done((f32[64,128]{1,0:T(8,128)S(1)}, f32[64,128]{1,0:T(8,128)S(1)}, u32[]{:S(2)}, u32[]{:S(2)}) %collective-permute-start.2) | collective-permute-done | bytes 32800 | tf_op jit(solution)/shard_map/ppermute | solution.py:50
  16.0 2.0 %collective-permute-start.10 = (f32[80,3968]{1,0:T(8,128)S(1)}, f32[80,3968]{1,0:T(8,128)S(1)}, u32[]{:S(2)}, u32[]{:S(2)}) collective-permute-start(f32[80,3968]{1,0:T(8,128)S(1)} %passed_on.6.refs_4_), channel_id=1, source_target_pairs={{0,2},{2,0},{1,3},{3,1},{4,6},{6,4},{5,7},{7,5},{8,10},{10,8},{9,1... | collective-permute-start | bytes 3809288 | tf_op jit(solution)/shard_map/ppermute | solution.py:50
  18.0 3.6 %collective-permute-start.6 = (f32[64,128]{1,0:T(8,128)S(1)}, f32[64,128]{1,0:T(8,128)S(1)}, u32[]{:S(2)}, u32[]{:S(2)}) collective-permute-start(f32[64,128]{1,0:T(8,128)S(1)} %total.8.refs_0_), channel_id=1, source_target_pairs={{0,24},{2,26},{4,28},{6,30},{8,16},{10,18},{12,20},{14,22},{16,8},... | collective-permute-start | bytes 98312 | tf_op jit(solution)/shard_map/ppermute | solution.py:50
  21.6 0.0 collective-permute-start.5
  21.6 0.8 %collective-permute-start.4 = (f32[64,128]{1,0:T(8,128)S(1)}, f32[64,128]{1,0:T(8,128)S(1)}, u32[]{:S(2)}, u32[]{:S(2)}) collective-permute-start(f32[64,128]{1,0:T(8,128)S(1)} %total.8.refs_0_), channel_id=1, source_target_pairs={{0,8},{2,10},{4,12},{6,14},{8,0},{10,2},{12,4},{14,6},{16,24},{18,... | collective-permute-start | bytes 98312 | tf_op jit(solution)/shard_map/ppermute | solution.py:50
  22.4 1.3 %collective-permute-done.6.refs_3_ = f32[64,128]{1,0:T(8,128)S(1)} collective-permute-done((f32[64,128]{1,0:T(8,128)S(1)}, f32[64,128]{1,0:T(8,128)S(1)}, u32[]{:S(2)}, u32[]{:S(2)}) %collective-permute-start.6) | collective-permute-done | bytes 32800 | tf_op jit(solution)/shard_map/ppermute | solution.py:50
  23.7 2.7 %collective-permute-done.5.refs_2_ = f32[64,128]{1,0:T(8,128)S(1)} collective-permute-done((f32[64,128]{1,0:T(8,128)S(1)}, f32[64,128]{1,0:T(8,128)S(1)}, u32[]{:S(2)}, u32[]{:S(2)}) %collective-permute-start.5) | collective-permute-done | bytes 32800 | tf_op jit(solution)/shard_map/ppermute | solution.py:50
  26.4 0.0 collective-permute-done.4.refs_1_
  26.4 0.1 collective-permute-start.7
  26.5 0.0 collective-permute-done.8.rest_0_
  26.5 0.0 copy-start.3
  26.5 1.2 %collective-permute-done.7.other_ref = f32[64,128]{1,0:T(8,128)S(1)} collective-permute-done((f32[64,128]{1,0:T(8,128)S(1)}, f32[64,128]{1,0:T(8,128)S(1)}, u32[]{:S(2)}, u32[]{:S(2)}) %collective-permute-start.7) | collective-permute-done | bytes 32800 | tf_op jit(solution)/shard_map/ppermute | solution.py:50
  27.7 2.2 %right_terms.1 = (f32[512,128]{1,0:T(8,128)S(1)}, f32[512,128]{1,0:T(8,128)S(1)}) custom-call(s32[1]{0:T(128)} %bitcast.1.me_ref, bf16[512,3968]{1,0:T(8,128)(2,1)S(1)} %bitcast.13, f32[128,3968]{1,0:T(8,128)S(1)} %bitcast.15, f32[64,128]{1,0:T(8,128)S(1)} %total.9.own_ref, f32[64,128]{1,0:T(8,128)S(1)} %collective-permute-done.7.other_ref, ...), custom_call_target="tpu_custom_call" | custom-call | tf_op jit(solution)/shard_map/right_terms/pallas_call | solution.py:280
  29.9 0.0 copy-done.3
  29.9 0.2 collective-permute-start.9
  30.1 3.5 %inverse_factor.1.refs_2_.both_ref = bf16[160,192]{1,0:T(8,128)(2,1)S(1)} custom-call(s32[1]{0:T(128)} %bitcast.1.me_ref, f32[64,128]{1,0:T(8,128)S(1)} %total.9.own_ref, f32[64,128]{1,0:T(8,128)S(1)} %collective-permute-done.7.other_ref, f32[512,128]{1,0:T(8,128)S(1)} %get-tuple-element.21.rest_0_), custom_call_target="tpu_custom_call" | custom-call | tf_op jit(solution)/shard_map/inverse_factor/pallas_call | solution.py:377
  33.6 0.0 collective-permute-done.9.refs_1_
  33.7 13.5 %all_to_all.10.p_ref = f32[8,64,128]{2,1,0:T(8,128)S(1)} all-to-all(f32[8,64,128]{2,1,0:T(8,128)S(1)} %bitcast.16), channel_id=1, replica_groups=mesh['rep'=8,'y'=2,'core'=2] {'rep'}, dimensions={0} | all-to-all | bytes 524288 | tf_op jit(solution)/shard_map/all_to_all | solution.py:64
  47.1 0.0 collective-permute-done.10.rest_0_
  47.2 0.6 collective-permute-start.11
  47.7 1.5 %collective-permute-start.13 = (f32[48,3968]{1,0:T(8,128)}, f32[48,3968]{1,0:T(8,128)}, u32[]{:S(2)}, u32[]{:S(2)}) collective-permute-start(f32[48,3968]{1,0:T(8,128)} %passed_on.8.refs_2_), channel_id=1, source_target_pairs={{0,2},{2,0},{1,3},{3,1},{4,6},{6,4},{5,7},{7,5},{8,10},{10,8},{9,1... | collective-permute-start | bytes 2285576 | tf_op jit(solution)/shard_map/ppermute | solution.py:50
  49.3 2.3 %collective-permute-done.11.refs_1_ = f32[64,128]{1,0:T(8,128)S(1)} collective-permute-done((f32[64,128]{1,0:T(8,128)S(1)}, f32[64,128]{1,0:T(8,128)S(1)}, u32[]{:S(2)}, u32[]{:S(2)}) %collective-permute-start.11) | collective-permute-done | bytes 32800 | tf_op jit(solution)/shard_map/ppermute | solution.py:50
  51.6 0.7 %total.11 = f32[8,64,128]{2,1,0:T(8,128)} custom-call(f32[64,128]{1,0:T(8,128)S(1)} %sum_parts.1.refs_1_.refs_0_, f32[64,128]{1,0:T(8,128)S(1)} %collective-permute-done.11.refs_1_, f32[48,3968]{1,0:T(8,128)} %passed_on.8.refs_2_), custom_call_target="tpu_custom_call" | custom-call | tf_op jit(solution)/shard_map/total/pallas_call | solution.py:86
  52.3 4.2 %all-to-all-start.1 = ((f32[8,64,128]{2,1,0:T(8,128)}), f32[8,64,128]{2,1,0:T(8,128)}, u32[]{:S(2)}, u32[]{:S(2)}) async-start(f32[8,64,128]{2,1,0:T(8,128)} %total.11), calls=%async_computation.1 | async-start | bytes 524288 | tf_op jit(solution)/shard_map/all_to_all | solution.py:64
  56.4 2.7 %fusion.refs_1_.p_ref = f32[128,3968]{1,0:T(8,128)S(1)} fusion(f32[128,3968]{1,0:T(8,128)} %copy-done.3, bf16[1,1,512,3968]{3,2,1,0:T(8,128)(2,1)} %param.3, s32[]{:T(128)S(6)} %select_n.3, f32[1,128,3968]{2,1,0:T(8,128)} %param.4), kind=kLoop, calls=%fused_computation.1 | loop fusion | flops 1523712 | bytes 7110660 | tf_op jit(solution)/shard_map/add | solution.py:444
  59.2 5.6 %all-to-all-done.1 = f32[8,64,128]{2,1,0:T(8,128)} async-done(((f32[8,64,128]{2,1,0:T(8,128)}), f32[8,64,128]{2,1,0:T(8,128)}, u32[]{:S(2)}, u32[]{:S(2)}) %all-to-all-start.1) | async-done | bytes 262176 | tf_op jit(solution)/shard_map/all_to_all | solution.py:64
  64.8 0.0 collective-permute-start.12
  64.8 1.7 %collective-permute-done.12.other_ref = f32[512,128]{1,0:T(8,128)S(1)} collective-permute-done((f32[512,128]{1,0:T(8,128)}, f32[512,128]{1,0:T(8,128)S(1)}, u32[]{:S(2)}, u32[]{:S(2)}) %collective-permute-start.12) | collective-permute-done | bytes 262176 | tf_op jit(solution)/shard_map/ppermute | solution.py:50
  66.5 0.0 collective-permute-done.13.rest_1_
  66.5 4.2 %finish.1 = (f32[128,3968]{1,0:T(8,128)}, f32[128,3968]{1,0:T(8,128)}, f32[32,3968]{1,0:T(8,128)}) custom-call(s32[1]{0:T(128)} %bitcast.core_ref, bf16[160,192]{1,0:T(8,128)(2,1)S(1)} %inverse_factor.1.refs_2_.both_ref, f32[512,128]{1,0:T(8,128)} %passed_on.9.own_ref, f32[512,128]{1,0:T(8,128)S(1)} %collective-permute-done.12.other_ref, ...), custom_call_target="tpu_custom_call" | custom-call | tf_op jit(solution)/shard_map/finish/pallas_call | solution.py:334
  (12 shorter events, 0.1 us)
Async XLA Ops:
  0.6 2.2 %copy-start = (bf16[1,1,512,3968]{3,2,1,0:T(8,128)(2,1)S(1)}, bf16[1,1,512,3968]{3,2,1,0:T(8,128)(2,1)}, u32[]{:S(2)}) copy-start(bf16[1,1,512,3968]{3,2,1,0:T(8,128)(2,1)} %param.3) | copy-start | bytes 12189700
  2.8 1.0 %copy-start.4 = (f32[32,3968]{1,0:T(8,128)S(1)}, f32[32,3968]{1,0:T(8,128)}, u32[]{:S(2)}) copy-start(f32[32,3968]{1,0:T(8,128)} %q_ref.1) | copy-start | bytes 1523716
  3.8 2.2 %copy-start.2 = (f32[1,128,3968]{2,1,0:T(8,128)S(1)}, f32[1,128,3968]{2,1,0:T(8,128)}, u32[]{:S(2)}) copy-start(f32[1,128,3968]{2,1,0:T(8,128)} %param.4) | copy-start | bytes 6094852
  5.5 1.4 %collective-permute-start = (f32[64,128]{1,0:T(8,128)S(1)}, f32[64,128]{1,0:T(8,128)S(1)}, u32[]{:S(2)}, u32[]{:S(2)}) collective-permute-start(f32[64,128]{1,0:T(8,128)S(1)} %get-tuple-element.16), channel_id=1, source_target_pairs={{0,1},{1,0},{2,3},{3,2},{4,5},{5,4},{6,7},{7,6},{8,9},{9,8},{10,11... | collective-permute-start | bytes 98312 | tf_op jit(solution)/shard_map/ppermute | solution.py:50
  6.9 7.2 %collective-permute-start.3 = (f32[128,3968]{1,0:T(8,128)S(1)}, f32[128,3968]{1,0:T(8,128)S(1)}, u32[]{:S(2)}, u32[]{:S(2)}) collective-permute-start(f32[128,3968]{1,0:T(8,128)S(1)} %passed_on.5), channel_id=1, source_target_pairs={{0,1},{1,0},{2,3},{3,2},{4,5},{5,4},{6,7},{7,6},{8,9},{9,8},{10,11... | collective-permute-start | bytes 6094856 | tf_op jit(solution)/shard_map/ppermute | solution.py:50
  7.3 4.6 %collective-permute-start.1 = (f32[64,128]{1,0:T(8,128)S(1)}, f32[64,128]{1,0:T(8,128)S(1)}, u32[]{:S(2)}, u32[]{:S(2)}) collective-permute-start(f32[64,128]{1,0:T(8,128)S(1)} %total.6.refs_0_.refs_1_), channel_id=1, source_target_pairs={{0,2},{2,0},{4,6},{6,4},{8,10},{10,8},{12,14},{14,12},{16,18},{18,... | collective-permute-start | bytes 98312 | tf_op jit(solution)/shard_map/ppermute | solution.py:50
  11.9 2.2 %copy-start.1 = (bf16[1,1,512,3968]{3,2,1,0:T(8,128)(2,1)S(1)}, bf16[1,1,512,3968]{3,2,1,0:T(8,128)(2,1)}, u32[]{:S(2)}) copy-start(bf16[1,1,512,3968]{3,2,1,0:T(8,128)(2,1)} %param.3) | copy-start | bytes 12189700
  11.9 14.6 %collective-permute-start.8 = (f32[128,3968]{1,0:T(8,128)S(1)}, f32[128,3968]{1,0:T(8,128)S(1)}, u32[]{:S(2)}, u32[]{:S(2)}) collective-permute-start(f32[128,3968]{1,0:T(8,128)S(1)} %passed_on.7), channel_id=1, source_target_pairs={{0,1},{1,0},{2,3},{3,2},{4,5},{5,4},{6,7},{7,6},{8,9},{9,8},{10,11... | collective-permute-start | bytes 6094856 | tf_op jit(solution)/shard_map/ppermute | solution.py:50
  12.0 4.0 %collective-permute-start.2 = (f32[64,128]{1,0:T(8,128)S(1)}, f32[64,128]{1,0:T(8,128)S(1)}, u32[]{:S(2)}, u32[]{:S(2)}) collective-permute-start(f32[64,128]{1,0:T(8,128)S(1)} %total.7.refs_0_.refs_1_), channel_id=1, source_target_pairs={{0,4},{2,6},{4,0},{6,2},{8,12},{10,14},{12,8},{14,10},{16,20},{18,... | collective-permute-start | bytes 98312 | tf_op jit(solution)/shard_map/ppermute | solution.py:50
  16.0 31.1 %collective-permute-start.10 = (f32[80,3968]{1,0:T(8,128)S(1)}, f32[80,3968]{1,0:T(8,128)S(1)}, u32[]{:S(2)}, u32[]{:S(2)}) collective-permute-start(f32[80,3968]{1,0:T(8,128)S(1)} %passed_on.6.refs_4_), channel_id=1, source_target_pairs={{0,2},{2,0},{1,3},{3,1},{4,6},{6,4},{5,7},{7,5},{8,10},{10,8},{9,1... | collective-permute-start | bytes 3809288 | tf_op jit(solution)/shard_map/ppermute | solution.py:50
  18.0 5.7 %collective-permute-start.6 = (f32[64,128]{1,0:T(8,128)S(1)}, f32[64,128]{1,0:T(8,128)S(1)}, u32[]{:S(2)}, u32[]{:S(2)}) collective-permute-start(f32[64,128]{1,0:T(8,128)S(1)} %total.8.refs_0_), channel_id=1, source_target_pairs={{0,24},{2,26},{4,28},{6,30},{8,16},{10,18},{12,20},{14,22},{16,8},... | collective-permute-start | bytes 98312 | tf_op jit(solution)/shard_map/ppermute | solution.py:50
  21.6 4.8 %collective-permute-start.5 = (f32[64,128]{1,0:T(8,128)S(1)}, f32[64,128]{1,0:T(8,128)S(1)}, u32[]{:S(2)}, u32[]{:S(2)}) collective-permute-start(f32[64,128]{1,0:T(8,128)S(1)} %total.8.refs_0_), channel_id=1, source_target_pairs={{0,16},{2,18},{4,20},{6,22},{8,24},{10,26},{12,28},{14,30},{16,0},... | collective-permute-start | bytes 98312 | tf_op jit(solution)/shard_map/ppermute | solution.py:50
  21.6 4.8 %collective-permute-start.4 = (f32[64,128]{1,0:T(8,128)S(1)}, f32[64,128]{1,0:T(8,128)S(1)}, u32[]{:S(2)}, u32[]{:S(2)}) collective-permute-start(f32[64,128]{1,0:T(8,128)S(1)} %total.8.refs_0_), channel_id=1, source_target_pairs={{0,8},{2,10},{4,12},{6,14},{8,0},{10,2},{12,4},{14,6},{16,24},{18,... | collective-permute-start | bytes 98312 | tf_op jit(solution)/shard_map/ppermute | solution.py:50
  26.4 1.3 %collective-permute-start.7 = (f32[64,128]{1,0:T(8,128)S(1)}, f32[64,128]{1,0:T(8,128)S(1)}, u32[]{:S(2)}, u32[]{:S(2)}) collective-permute-start(f32[64,128]{1,0:T(8,128)S(1)} %total.9.own_ref), channel_id=1, source_target_pairs={{0,1},{1,0},{2,3},{3,2},{4,5},{5,4},{6,7},{7,6},{8,9},{9,8},{10,11... | collective-permute-start | bytes 98312 | tf_op jit(solution)/shard_map/ppermute | solution.py:50
  26.5 3.4 %copy-start.3 = (f32[128,3968]{1,0:T(8,128)}, f32[128,3968]{1,0:T(8,128)S(1)}, u32[]{:S(2)}) copy-start(f32[128,3968]{1,0:T(8,128)S(1)} %collective-permute-done.8.rest_0_) | copy-start | bytes 6094852
  29.9 3.8 %collective-permute-start.9 = (f32[512,128]{1,0:T(8,128)S(1)}, f32[512,128]{1,0:T(8,128)S(1)}, u32[]{:S(2)}, u32[]{:S(2)}) collective-permute-start(f32[512,128]{1,0:T(8,128)S(1)} %get-tuple-element.21.rest_0_), channel_id=1, source_target_pairs={{0,1},{1,0},{2,3},{3,2},{4,5},{5,4},{6,7},{7,6},{8,9},{9,8},{10,11... | collective-permute-start | bytes 786440 | tf_op jit(solution)/shard_map/ppermute | solution.py:50
  47.2 4.4 %collective-permute-start.11 = (f32[64,128]{1,0:T(8,128)S(1)}, f32[64,128]{1,0:T(8,128)S(1)}, u32[]{:S(2)}, u32[]{:S(2)}) collective-permute-start(f32[64,128]{1,0:T(8,128)S(1)} %sum_parts.1.refs_1_.refs_0_), channel_id=1, source_target_pairs={{0,2},{2,0},{1,3},{3,1},{4,6},{6,4},{5,7},{7,5},{8,10},{10,8},{9,1... | collective-permute-start | bytes 98312 | tf_op jit(solution)/shard_map/ppermute | solution.py:50
  47.7 18.8 %collective-permute-start.13 = (f32[48,3968]{1,0:T(8,128)}, f32[48,3968]{1,0:T(8,128)}, u32[]{:S(2)}, u32[]{:S(2)}) collective-permute-start(f32[48,3968]{1,0:T(8,128)} %passed_on.8.refs_2_), channel_id=1, source_target_pairs={{0,2},{2,0},{1,3},{3,1},{4,6},{6,4},{5,7},{7,5},{8,10},{10,8},{9,1... | collective-permute-start | bytes 2285576 | tf_op jit(solution)/shard_map/ppermute | solution.py:50
  52.3 12.5 %all-to-all-start.1 = ((f32[8,64,128]{2,1,0:T(8,128)}), f32[8,64,128]{2,1,0:T(8,128)}, u32[]{:S(2)}, u32[]{:S(2)}) async-start(f32[8,64,128]{2,1,0:T(8,128)} %total.11), calls=%async_computation.1 | async-start | bytes 524288 | tf_op jit(solution)/shard_map/all_to_all | solution.py:64
  64.8 1.7 %collective-permute-start.12 = (f32[512,128]{1,0:T(8,128)}, f32[512,128]{1,0:T(8,128)S(1)}, u32[]{:S(2)}, u32[]{:S(2)}) collective-permute-start(f32[512,128]{1,0:T(8,128)} %passed_on.9.own_ref), channel_id=1, source_target_pairs={{0,1},{1,0},{2,3},{3,2},{4,5},{5,4},{6,7},{7,6},{8,9},{9,8},{10,11... | collective-permute-start | bytes 786440 | tf_op jit(solution)/shard_map/ppermute | solution.py:50

commit v3 on v2

--- a/solution.py
+++ b/solution.py
@@ -57,7 +57,6 @@
 ANYWHERE = pl.BlockSpec(memory_space=pl.ANY)
 VMEM = pl.BlockSpec(memory_space=pltpu.VMEM)
 SMEM = pl.BlockSpec(memory_space=pltpu.SMEM)
-HBM = pl.BlockSpec(memory_space=pltpu.HBM)
 
 
 def exchange(parts, axes):
@@ -152,9 +151,11 @@
     def kernel(where_ref, g_ref, a_ref, *rest):
         outs = rest[len(after) :]
         first = pl.multiple_of(where_ref[0] * block, block)
-        for (at, n), out in zip(cuts, outs):
-            rows = pl.ds(pl.multiple_of(first + at, 16), n)
-            out[...] = g_ref[rows, :].astype(F32) + a_ref[at : at + n, :]
+        for col, width in spans(cols, WIDE):
+            c = slice(col, col + width)
+            value = g_ref[pl.ds(first, block), c].astype(F32)
+            for (at, n), out in zip(cuts, outs):
+                out[:, c] = value[at : at + n] + a_ref[at : at + n, c]
 
     return pl.pallas_call(
         kernel,
@@ -294,7 +295,6 @@
     rank = both.shape[0] - rows
     per = WIDE // LANES
     parts = spans(cols, WIDE)
-    row_parts = spans(rows, 32)
     n_half = q_own.shape[0] // (per * rank)
     counts = [a.shape[0] for a in arrived]
     n_arrived = len(arrived)
@@ -304,30 +304,36 @@
         approx_ref, error_ref, q_ref, o_buf, n_buf, q_buf, sems = rest[n_arrived:]
         out = []
         left = both_ref[...]
-        for k, (at, n) in enumerate(parts):
-            c = slice(at, at + n)
+
+        def product(k):
+            n = parts[k][1]
             at_rows = slice((k % n_half) * per * rank, (k % n_half + 1) * per * rank)
             mine = core_ref[0] == k // n_half
             stacked = jnp.where(mine, own_ref[at_rows, :], other_ref[at_rows, :])
             q_sum = jnp.concatenate(
                 [stacked[b * rank : (b + 1) * rank] for b in range(n // LANES)], axis=1
             )
-            value = dot(left, six(q_sum, 0, False), ((1,), (0,)))
+            return dot(left, six(q_sum, 0, False), ((1,), (0,)))
+
+        later = product(0)
+        for k, (at, n) in enumerate(parts):
+            value = later
+            if k + 1 < len(parts):
+                later = product(k + 1)
+            c = slice(at, at + n)
             q_buf[:, c] = value[:rank]
             o_buf[:, c] = value[rank:]
-        out.append(started(q_buf, q_ref, sems.at[0, 0]))
-        for k, (at, n) in enumerate(row_parts):
-            r = pl.ds(at, n)
-            out.append(started(o_buf.at[r, :], approx_ref.at[r, :], sems.at[1, k]))
-        first = 0
-        for count, a_ref in zip(counts, a_refs):
-            for at, n in spans(count, 16):
-                r = slice(first + at, first + at + n)
-                n_buf[r, :] = (p_ref[r, :] + a_ref[at : at + n, :]) - o_buf[r, :]
-                rows_out = pl.ds(first + at, n)
-                k = (first + at) // 16
-                out.append(started(n_buf.at[rows_out, :], error_ref.at[rows_out, :], sems.at[2, k]))
-            first += count
+            first = 0
+            for count, a_ref in zip(counts, a_refs):
+                r = slice(first, first + count)
+                n_buf[r, c] = (p_ref[r, c] + a_ref[:, c]) - value[rank + first : rank + first + count]
+                first += count
+            for i, (buf, ref) in enumerate(
+                ((o_buf, approx_ref), (n_buf, error_ref), (q_buf, q_ref))
+            ):
+                out.append(
+                    started(buf.at[:, pl.ds(at, n)], ref.at[:, pl.ds(at, n)], sems.at[i, k])
+                )
         for copy in out:
             copy.wait()
 
@@ -343,7 +349,7 @@
         scratch_shapes=[pltpu.VMEM((rows, cols), F32)] * 2
         + [
             pltpu.VMEM((rank, cols), F32),
-            pltpu.SemaphoreType.DMA((3, -(-rows // 16))),
+            pltpu.SemaphoreType.DMA((3, len(parts))),
         ],
         compiler_params=params(),
         cost_estimate=NO_COST,
@@ -364,10 +370,10 @@
         unit = jnp.where(col == row + rank, 1.0, 0.0).astype(F32)
         w = jnp.concatenate([gram, jnp.zeros_like(gram)], axis=1) + unit
         for k in range(rank):
-            column = w[:, k : k + 1] * (1.0 / w[k : k + 1, k : k + 1])
-            w = jnp.where(row > k, w - column * w[k : k + 1, :], w)
-        pivots = jnp.sum(jnp.where(row == col, w, 0.0), axis=1, keepdims=True)
-        w = w * (1.0 / jnp.sqrt(pivots))
+            scale = 1.0 / jnp.sqrt(w[k : k + 1, k : k + 1])
+            pivot = w[k : k + 1, :] * scale
+            column = w[:, k : k + 1] * scale
+            w = jnp.where(row > k, w - column * pivot, jnp.where(row == k, pivot, w))
         inverse = w[:, rank:]
         basis = dot(inverse, f_all[me_ref[0]], ((1,), (0,)), lax.Precision.HIGHEST)
         to_approx = dot(basis.T, inverse, ((1,), (0,)), lax.Precision.HIGHEST)
@@ -381,7 +387,7 @@
         out_specs=VMEM,
         scratch_shapes=[pltpu.VMEM((n_shard, rank, block), F32)],
         compiler_params=params(),
-        cost_estimate=NO_COST,
+        cost_estimate=pl.CostEstimate(flops=0, bytes_accessed=1 << 24, transcendentals=0),
         name="inverse_factor",
     )(me, *halves, *after)
 
@@ -408,7 +414,7 @@
     chips = ("rep", "y")
     n_bits = (n_rep * n_y).bit_length() - 1
     distances = range(1, n_y)
-    cuts = [(0, 80), (80, block - 80)]
+    cuts = [(0, 72), (72, block - 72)]
 
     send, keep, q_columns, own_wide, *wide = left_terms(me, grads, q_factor, n_shard)
     from_other = partner(send, "core", 1)
@@ -433,10 +439,10 @@
     halves = [half, partner(half, "core", 1)]
 
     send, keep = right_terms(me, grads, error, halves, rank, n_shard, [from_core])
-    both = inverse_factor(me, halves, rank, n_rep, n_shard, [send])
-    own_half = total([keep, partner(send, "core", 1)], [both])
+    own_half = total([keep, partner(send, "core", 1)])
+    both = inverse_factor(me, halves, rank, n_rep, n_shard, [own_half])
     parts = exchange(own_half.reshape(n_rep, -1, LANES), "rep")
-    piece = sum_parts(parts, [first_part])
+    piece = sum_parts(parts, [first_part, both])
     values, second_part = over_y(1, [piece])
     piece = [piece] + [partner(piece, "y", d) for d in distances]
     pieces_out = total(piece, values, n_rep)

time: 71.1 us -> 70.8 us (level)
  blocking collectives: 13.5 us -> 0 us
  waiting for transfers between devices: 17.7 us -> 26.6 us
  starting transfers between devices: 18.6 us -> 22.2 us
    all_to_all x1 -> x0, blocking collectives: 13.5 us -> none  [exchange(): return lax.all_to_all(parts, axes, split_axis=0, concat_axis=0, tiled=True)]
    all_to_all x1 -> x2, waiting for transfers between devices: 5.58 us -> 10.8 us  [exchange(): return lax.all_to_all(parts, axes, split_axis=0, concat_axis=0, tiled=True)]
    ppermute x14, waiting for transfers between devices: 12.2 us -> 15.8 us  [partner(): lax.ppermute(x, axis, [(i, i ^ d) for i in range(lax.axis_size(axis))])]
    all_to_all x1 -> x2, starting transfers between devices: 4.15 us -> 7.75 us  [exchange(): return lax.all_to_all(parts, axes, split_axis=0, concat_axis=0, tiled=True)]
  transfers between devices with their start and end apart: 15 -> 16, of which waited for: 9 -> 12; matrix products, arithmetic and copies ran while one was open for 4% -> 4% of each run, Pallas kernels for 12% -> 13%
where the time goes in v3:
time: 70.8 us; the launch traced here: 70.3 us
  waiting for transfers between devices  26.6 us (38%)
  starting transfers between devices  22.2 us (31%)
  Pallas kernels  14.8 us (21%)
  local copies, waits for them, and re-layouts  3.2 us (5%)
  other arithmetic  2.74 us (4%)
  between operations  0.75 us (1%)
    ppermute x14, waiting for transfers between devices, partner(): lax.ppermute(x, axis, [(i, i ^ d) for i in range(lax.axis_size(axis))])  15.8 us
    ppermute x14, starting transfers between devices, partner(): lax.ppermute(x, axis, [(i, i ^ d) for i in range(lax.axis_size(axis))])  14.5 us
    all_to_all x2, waiting for transfers between devices, exchange(): return lax.all_to_all(parts, axes, split_axis=0, concat_axis=0, tiled=True)  10.8 us
    all_to_all x2, starting transfers between devices, exchange(): return lax.all_to_all(parts, axes, split_axis=0, concat_axis=0, tiled=True)  7.75 us
    pallas_call x1, Pallas kernels, inverse_factor(): pl.pallas_call(kernel, out_shape=jax.ShapeDtypeStruct((rank + block, 6 *...  3.93 us
    pallas_call x1, Pallas kernels, finish(): pl.pallas_call(kernel, out_shape=[jax.ShapeDtypeStruct((rows, cols), F32)...  3.69 us
    unnamed x10, local copies, waits for them, and re-layouts  3.2 us
    add x1, other arithmetic, body(): partial = own_terms + from_core + error  2.74 us
  transfers between devices with their start and end apart: 16, of which 12 were waited for; matrix products, arithmetic and copies ran while one was open for 4% of the time, Pallas kernels for 13%

profile of v3, /device:TPU:0, one launch (start us, length us, event | category | flops | bytes accessed | tf_op | source)
XLA Modules:
  0.0 70.3 jit_solution(17228326452563321328)
XLA Ops:
  0.6 0.0 copy-start
  0.6 2.1 %copy-done = bf16[1,1,512,3968]{3,2,1,0:T(8,128)(2,1)S(1)} copy-done((bf16[1,1,512,3968]{3,2,1,0:T(8,128)(2,1)S(1)}, bf16[1,1,512,3968]{3,2,1,0:T(8,128)(2,1)}, u32[]{:S(2)}) %copy-start) | copy-done | bytes 4063256
  2.8 1.0 %copy-done.4 = f32[32,3968]{1,0:T(8,128)S(1)} copy-done((f32[32,3968]{1,0:T(8,128)S(1)}, f32[32,3968]{1,0:T(8,128)}, u32[]{:S(2)}) %copy-start.4) | copy-done | bytes 507928
  3.8 1.6 %left_terms.1 = (f32[64,128]{1,0:T(8,128)S(1)}, f32[64,128]{1,0:T(8,128)S(1)}, bf16[3968,128]{1,0:T(8,128)(2,1)S(1)}, f32[128,3968]{1,0:T(8,128)S(1)}, f32[128,3968]{1,0:T(8,128)S(1)}) custom-call(s32[1]{0:T(128)} %bitcast.1.me_ref, bf16[512,3968]{1,0:T(8,128)(2,1)S(1)} %bitcast.11, f32[32,3968]{1,0:T(8,128)S(1)} %copy-done.4), custom_call_target="tpu_custom_call" | custom-call | tf_op jit(solution)/shard_map/left_terms/pallas_call | solution.py:200
  5.5 0.5 collective-permute-start
  6.0 0.0 copy-done.2
  6.0 0.8 %error_term.1.refs_2_ = f32[64,128]{1,0:T(8,128)S(1)} custom-call(s32[1]{0:T(128)} %bitcast.1.me_ref, f32[128,3968]{1,0:T(8,128)S(1)} %bitcast.14, bf16[3968,128]{1,0:T(8,128)(2,1)S(1)} %get-tuple-element.17.q_ref), custom_call_target="tpu_custom_call" | custom-call | tf_op jit(solution)/shard_map/error_term/pallas_call | solution.py:231
  6.8 0.1 collective-permute-done.refs_1_
  6.9 0.4 collective-permute-start.3
  7.3 2.7 %collective-permute-start.1 = (f32[64,128]{1,0:T(8,128)S(1)}, f32[64,128]{1,0:T(8,128)S(1)}, u32[]{:S(2)}, u32[]{:S(2)}) collective-permute-start(f32[64,128]{1,0:T(8,128)S(1)} %total.6.refs_0_.refs_1_), channel_id=1, source_target_pairs={{0,2},{2,0},{4,6},{6,4},{8,10},{10,8},{12,14},{14,12},{16,18},{18,... | collective-permute-start | bytes 98312 | tf_op jit(solution)/shard_map/ppermute | solution.py:50
  10.0 1.9 %collective-permute-done.1.refs_1_ = f32[64,128]{1,0:T(8,128)S(1)} collective-permute-done((f32[64,128]{1,0:T(8,128)S(1)}, f32[64,128]{1,0:T(8,128)S(1)}, u32[]{:S(2)}, u32[]{:S(2)}) %collective-permute-start.1) | collective-permute-done | bytes 32800 | tf_op jit(solution)/shard_map/ppermute | solution.py:50
  11.9 0.1 collective-permute-start.8
  12.0 2.1 %collective-permute-start.2 = (f32[64,128]{1,0:T(8,128)S(1)}, f32[64,128]{1,0:T(8,128)S(1)}, u32[]{:S(2)}, u32[]{:S(2)}) collective-permute-start(f32[64,128]{1,0:T(8,128)S(1)} %total.7.refs_0_.refs_1_), channel_id=1, source_target_pairs={{0,4},{2,6},{4,0},{6,2},{8,12},{10,14},{12,8},{14,10},{16,20},{18,... | collective-permute-start | bytes 98312 | tf_op jit(solution)/shard_map/ppermute | solution.py:50
  14.0 0.0 collective-permute-done.3.a_ref
  14.0 0.0 copy-done.1
  14.0 1.1 %add_rows.1 = (f32[72,3968]{1,0:T(8,128)S(1)}, f32[56,3968]{1,0:T(8,128)}) custom-call(s32[1]{0:T(128)S(6)} %xor.3.where_ref, bf16[512,3968]{1,0:T(8,128)(2,1)S(1)} %bitcast.12, f32[128,3968]{1,0:T(8,128)S(1)} %collective-permute-done.3.a_ref), custom_call_target="tpu_custom_call" | custom-call | tf_op jit(solution)/shard_map/add_rows/pallas_call | solution.py:160
  15.1 0.8 %collective-permute-done.2.refs_1_ = f32[64,128]{1,0:T(8,128)S(1)} collective-permute-done((f32[64,128]{1,0:T(8,128)S(1)}, f32[64,128]{1,0:T(8,128)S(1)}, u32[]{:S(2)}, u32[]{:S(2)}) %collective-permute-start.2) | collective-permute-done | bytes 32800 | tf_op jit(solution)/shard_map/ppermute | solution.py:50
  16.0 2.0 %collective-permute-start.10 = (f32[72,3968]{1,0:T(8,128)S(1)}, f32[72,3968]{1,0:T(8,128)S(1)}, u32[]{:S(2)}, u32[]{:S(2)}) collective-permute-start(f32[72,3968]{1,0:T(8,128)S(1)} %passed_on.6.refs_4_), channel_id=1, source_target_pairs={{0,2},{2,0},{1,3},{3,1},{4,6},{6,4},{5,7},{7,5},{8,10},{10,8},{9,1... | collective-permute-start | bytes 3428360 | tf_op jit(solution)/shard_map/ppermute | solution.py:50
  18.0 3.6 %collective-permute-start.6 = (f32[64,128]{1,0:T(8,128)S(1)}, f32[64,128]{1,0:T(8,128)S(1)}, u32[]{:S(2)}, u32[]{:S(2)}) collective-permute-start(f32[64,128]{1,0:T(8,128)S(1)} %total.8.refs_0_), channel_id=1, source_target_pairs={{0,24},{2,26},{4,28},{6,30},{8,16},{10,18},{12,20},{14,22},{16,8},... | collective-permute-start | bytes 98312 | tf_op jit(solution)/shard_map/ppermute | solution.py:50
  21.6 0.0 collective-permute-start.5
  21.6 0.8 %collective-permute-start.4 = (f32[64,128]{1,0:T(8,128)S(1)}, f32[64,128]{1,0:T(8,128)S(1)}, u32[]{:S(2)}, u32[]{:S(2)}) collective-permute-start(f32[64,128]{1,0:T(8,128)S(1)} %total.8.refs_0_), channel_id=1, source_target_pairs={{0,8},{2,10},{4,12},{6,14},{8,0},{10,2},{12,4},{14,6},{16,24},{18,... | collective-permute-start | bytes 98312 | tf_op jit(solution)/shard_map/ppermute | solution.py:50
  22.4 1.3 %collective-permute-done.6.refs_3_ = f32[64,128]{1,0:T(8,128)S(1)} collective-permute-done((f32[64,128]{1,0:T(8,128)S(1)}, f32[64,128]{1,0:T(8,128)S(1)}, u32[]{:S(2)}, u32[]{:S(2)}) %collective-permute-start.6) | collective-permute-done | bytes 32800 | tf_op jit(solution)/shard_map/ppermute | solution.py:50
  23.7 2.7 %collective-permute-done.5.refs_2_ = f32[64,128]{1,0:T(8,128)S(1)} collective-permute-done((f32[64,128]{1,0:T(8,128)S(1)}, f32[64,128]{1,0:T(8,128)S(1)}, u32[]{:S(2)}, u32[]{:S(2)}) %collective-permute-start.5) | collective-permute-done | bytes 32800 | tf_op jit(solution)/shard_map/ppermute | solution.py:50
  26.4 0.0 collective-permute-done.4.refs_1_
  26.4 0.1 collective-permute-start.7
  26.5 0.0 collective-permute-done.8.rest_0_
  26.5 0.0 copy-start.3
  26.5 1.2 %collective-permute-done.7.other_ref = f32[64,128]{1,0:T(8,128)S(1)} collective-permute-done((f32[64,128]{1,0:T(8,128)S(1)}, f32[64,128]{1,0:T(8,128)S(1)}, u32[]{:S(2)}, u32[]{:S(2)}) %collective-permute-start.7) | collective-permute-done | bytes 32800 | tf_op jit(solution)/shard_map/ppermute | solution.py:50
  27.7 2.1 %right_terms.1 = (f32[512,128]{1,0:T(8,128)S(1)}, f32[512,128]{1,0:T(8,128)S(1)}) custom-call(s32[1]{0:T(128)} %bitcast.1.me_ref, bf16[512,3968]{1,0:T(8,128)(2,1)S(1)} %bitcast.13, f32[128,3968]{1,0:T(8,128)S(1)} %bitcast.15, f32[64,128]{1,0:T(8,128)S(1)} %total.9.own_ref, f32[64,128]{1,0:T(8,128)S(1)} %collective-permute-done.7.other_ref, ...), custom_call_target="tpu_custom_call" | custom-call | tf_op jit(solution)/shard_map/right_terms/pallas_call | solution.py:281
  29.8 0.0 copy-done.3
  29.8 0.2 collective-permute-start.9
  30.1 1.4 %collective-permute-done.9.refs_1_ = f32[512,128]{1,0:T(8,128)S(1)} collective-permute-done((f32[512,128]{1,0:T(8,128)S(1)}, f32[512,128]{1,0:T(8,128)S(1)}, u32[]{:S(2)}, u32[]{:S(2)}) %collective-permute-start.9) | collective-permute-done | bytes 262176 | tf_op jit(solution)/shard_map/ppermute | solution.py:50
  31.4 0.7 %total.10.rest_0_ = f32[512,128]{1,0:T(8,128)} custom-call(f32[512,128]{1,0:T(8,128)S(1)} %get-tuple-element.21.refs_0_, f32[512,128]{1,0:T(8,128)S(1)} %collective-permute-done.9.refs_1_), custom_call_target="tpu_custom_call" | custom-call | tf_op jit(solution)/shard_map/total/pallas_call | solution.py:85
  32.2 4.2 %all-to-all-start = ((f32[8,64,128]{2,1,0:T(8,128)}), f32[8,64,128]{2,1,0:T(8,128)S(1)}, u32[]{:S(2)}, u32[]{:S(2)}) async-start(f32[8,64,128]{2,1,0:T(8,128)} %bitcast.4), calls=%async_computation | async-start | bytes 524288 | tf_op jit(solution)/shard_map/all_to_all | solution.py:63
  36.4 3.9 %inverse_factor.1.rest_1_.both_ref = bf16[160,192]{1,0:T(8,128)(2,1)S(1)} custom-call(s32[1]{0:T(128)} %bitcast.1.me_ref, f32[64,128]{1,0:T(8,128)S(1)} %total.9.own_ref, f32[64,128]{1,0:T(8,128)S(1)} %collective-permute-done.7.other_ref, f32[512,128]{1,0:T(8,128)} %total.10.rest_0_), custom_call_target="tpu_custom_call" | custom-call | bytes 16777216 | tf_op jit(solution)/shard_map/inverse_factor/pallas_call | solution.py:383
  40.3 5.3 %all-to-all-done.p_ref = f32[8,64,128]{2,1,0:T(8,128)S(1)} async-done(((f32[8,64,128]{2,1,0:T(8,128)}), f32[8,64,128]{2,1,0:T(8,128)S(1)}, u32[]{:S(2)}, u32[]{:S(2)}) %all-to-all-start) | async-done | bytes 262176 | tf_op jit(solution)/shard_map/all_to_all | solution.py:63
  45.6 0.0 collective-permute-done.10.rest_0_
  45.7 0.6 collective-permute-start.11
  46.2 1.5 %collective-permute-start.13 = (f32[56,3968]{1,0:T(8,128)}, f32[56,3968]{1,0:T(8,128)}, u32[]{:S(2)}, u32[]{:S(2)}) collective-permute-start(f32[56,3968]{1,0:T(8,128)} %passed_on.8.refs_2_), channel_id=1, source_target_pairs={{0,2},{2,0},{1,3},{3,1},{4,6},{6,4},{5,7},{7,5},{8,10},{10,8},{9,1... | collective-permute-start | bytes 2666504 | tf_op jit(solution)/shard_map/ppermute | solution.py:50
  47.7 2.3 %collective-permute-done.11.refs_1_ = f32[64,128]{1,0:T(8,128)S(1)} collective-permute-done((f32[64,128]{1,0:T(8,128)S(1)}, f32[64,128]{1,0:T(8,128)S(1)}, u32[]{:S(2)}, u32[]{:S(2)}) %collective-permute-start.11) | collective-permute-done | bytes 32800 | tf_op jit(solution)/shard_map/ppermute | solution.py:50
  50.0 0.7 %total.11 = f32[8,64,128]{2,1,0:T(8,128)} custom-call(f32[64,128]{1,0:T(8,128)S(1)} %sum_parts.1.refs_1_.refs_0_, f32[64,128]{1,0:T(8,128)S(1)} %collective-permute-done.11.refs_1_, f32[56,3968]{1,0:T(8,128)} %passed_on.8.refs_2_), custom_call_target="tpu_custom_call" | custom-call | tf_op jit(solution)/shard_map/total/pallas_call | solution.py:85
  50.8 3.5 %all-to-all-start.1 = ((f32[8,64,128]{2,1,0:T(8,128)}), f32[8,64,128]{2,1,0:T(8,128)S(1)}, u32[]{:S(2)}, u32[]{:S(2)}) async-start(f32[8,64,128]{2,1,0:T(8,128)} %total.11), calls=%async_computation.1 | async-start | bytes 524288 | tf_op jit(solution)/shard_map/all_to_all | solution.py:63
  54.3 2.7 %fusion.refs_1_.p_ref = f32[128,3968]{1,0:T(8,128)S(1)} fusion(f32[128,3968]{1,0:T(8,128)} %copy-done.3, bf16[1,1,512,3968]{3,2,1,0:T(8,128)(2,1)} %param.3, s32[]{:T(128)S(6)} %select_n.3, f32[1,128,3968]{2,1,0:T(8,128)} %param.4), kind=kLoop, calls=%fused_computation.1 | loop fusion | flops 1523712 | bytes 7110660 | tf_op jit(solution)/shard_map/add | solution.py:450
  57.0 5.5 %all-to-all-done.1 = f32[8,64,128]{2,1,0:T(8,128)S(1)} async-done(((f32[8,64,128]{2,1,0:T(8,128)}), f32[8,64,128]{2,1,0:T(8,128)S(1)}, u32[]{:S(2)}, u32[]{:S(2)}) %all-to-all-start.1) | async-done | bytes 262176 | tf_op jit(solution)/shard_map/all_to_all | solution.py:63
  62.5 0.0 collective-permute-start.12
  62.5 1.5 %collective-permute-done.12.other_ref = f32[512,128]{1,0:T(8,128)S(1)} collective-permute-done((f32[512,128]{1,0:T(8,128)S(1)}, f32[512,128]{1,0:T(8,128)S(1)}, u32[]{:S(2)}, u32[]{:S(2)}) %collective-permute-start.12) | collective-permute-done | bytes 262176 | tf_op jit(solution)/shard_map/ppermute | solution.py:50
  64.1 2.6 %collective-permute-done.13.rest_1_ = f32[56,3968]{1,0:T(8,128)} collective-permute-done((f32[56,3968]{1,0:T(8,128)}, f32[56,3968]{1,0:T(8,128)}, u32[]{:S(2)}, u32[]{:S(2)}) %collective-permute-start.13) | collective-permute-done | bytes 888864 | tf_op jit(solution)/shard_map/ppermute | solution.py:50
  66.6 3.7 %finish.1 = (f32[128,3968]{1,0:T(8,128)}, f32[128,3968]{1,0:T(8,128)}, f32[32,3968]{1,0:T(8,128)}) custom-call(s32[1]{0:T(128)} %bitcast.core_ref, bf16[160,192]{1,0:T(8,128)(2,1)S(1)} %inverse_factor.1.rest_1_.both_ref, f32[512,128]{1,0:T(8,128)S(1)} %passed_on.9.own_ref, f32[512,128]{1,0:T(8,128)S(1)} %collective-permute-done.12.other_ref, ...), custom_call_target="tpu_custom_call" | custom-call | tf_op jit(solution)/shard_map/finish/pallas_call | solution.py:340
  (13 shorter events, 0.1 us)
Async XLA Ops:
  0.6 2.2 %copy-start = (bf16[1,1,512,3968]{3,2,1,0:T(8,128)(2,1)S(1)}, bf16[1,1,512,3968]{3,2,1,0:T(8,128)(2,1)}, u32[]{:S(2)}) copy-start(bf16[1,1,512,3968]{3,2,1,0:T(8,128)(2,1)} %param.3) | copy-start | bytes 12189700
  2.8 1.0 %copy-start.4 = (f32[32,3968]{1,0:T(8,128)S(1)}, f32[32,3968]{1,0:T(8,128)}, u32[]{:S(2)}) copy-start(f32[32,3968]{1,0:T(8,128)} %q_ref.1) | copy-start | bytes 1523716
  3.8 2.2 %copy-start.2 = (f32[1,128,3968]{2,1,0:T(8,128)S(1)}, f32[1,128,3968]{2,1,0:T(8,128)}, u32[]{:S(2)}) copy-start(f32[1,128,3968]{2,1,0:T(8,128)} %param.4) | copy-start | bytes 6094852
  5.5 1.4 %collective-permute-start = (f32[64,128]{1,0:T(8,128)S(1)}, f32[64,128]{1,0:T(8,128)S(1)}, u32[]{:S(2)}, u32[]{:S(2)}) collective-permute-start(f32[64,128]{1,0:T(8,128)S(1)} %get-tuple-element.16), channel_id=1, source_target_pairs={{0,1},{1,0},{2,3},{3,2},{4,5},{5,4},{6,7},{7,6},{8,9},{9,8},{10,11... | collective-permute-start | bytes 98312 | tf_op jit(solution)/shard_map/ppermute | solution.py:50
  6.9 7.2 %collective-permute-start.3 = (f32[128,3968]{1,0:T(8,128)S(1)}, f32[128,3968]{1,0:T(8,128)S(1)}, u32[]{:S(2)}, u32[]{:S(2)}) collective-permute-start(f32[128,3968]{1,0:T(8,128)S(1)} %passed_on.5), channel_id=1, source_target_pairs={{0,1},{1,0},{2,3},{3,2},{4,5},{5,4},{6,7},{7,6},{8,9},{9,8},{10,11... | collective-permute-start | bytes 6094856 | tf_op jit(solution)/shard_map/ppermute | solution.py:50
  7.3 4.6 %collective-permute-start.1 = (f32[64,128]{1,0:T(8,128)S(1)}, f32[64,128]{1,0:T(8,128)S(1)}, u32[]{:S(2)}, u32[]{:S(2)}) collective-permute-start(f32[64,128]{1,0:T(8,128)S(1)} %total.6.refs_0_.refs_1_), channel_id=1, source_target_pairs={{0,2},{2,0},{4,6},{6,4},{8,10},{10,8},{12,14},{14,12},{16,18},{18,... | collective-permute-start | bytes 98312 | tf_op jit(solution)/shard_map/ppermute | solution.py:50
  11.9 2.2 %copy-start.1 = (bf16[1,1,512,3968]{3,2,1,0:T(8,128)(2,1)S(1)}, bf16[1,1,512,3968]{3,2,1,0:T(8,128)(2,1)}, u32[]{:S(2)}) copy-start(bf16[1,1,512,3968]{3,2,1,0:T(8,128)(2,1)} %param.3) | copy-start | bytes 12189700
  11.9 14.6 %collective-permute-start.8 = (f32[128,3968]{1,0:T(8,128)S(1)}, f32[128,3968]{1,0:T(8,128)S(1)}, u32[]{:S(2)}, u32[]{:S(2)}) collective-permute-start(f32[128,3968]{1,0:T(8,128)S(1)} %passed_on.7), channel_id=1, source_target_pairs={{0,1},{1,0},{2,3},{3,2},{4,5},{5,4},{6,7},{7,6},{8,9},{9,8},{10,11... | collective-permute-start | bytes 6094856 | tf_op jit(solution)/shard_map/ppermute | solution.py:50
  12.0 4.0 %collective-permute-start.2 = (f32[64,128]{1,0:T(8,128)S(1)}, f32[64,128]{1,0:T(8,128)S(1)}, u32[]{:S(2)}, u32[]{:S(2)}) collective-permute-start(f32[64,128]{1,0:T(8,128)S(1)} %total.7.refs_0_.refs_1_), channel_id=1, source_target_pairs={{0,4},{2,6},{4,0},{6,2},{8,12},{10,14},{12,8},{14,10},{16,20},{18,... | collective-permute-start | bytes 98312 | tf_op jit(solution)/shard_map/ppermute | solution.py:50
  16.0 29.6 %collective-permute-start.10 = (f32[72,3968]{1,0:T(8,128)S(1)}, f32[72,3968]{1,0:T(8,128)S(1)}, u32[]{:S(2)}, u32[]{:S(2)}) collective-permute-start(f32[72,3968]{1,0:T(8,128)S(1)} %passed_on.6.refs_4_), channel_id=1, source_target_pairs={{0,2},{2,0},{1,3},{3,1},{4,6},{6,4},{5,7},{7,5},{8,10},{10,8},{9,1... | collective-permute-start | bytes 3428360 | tf_op jit(solution)/shard_map/ppermute | solution.py:50
  18.0 5.7 %collective-permute-start.6 = (f32[64,128]{1,0:T(8,128)S(1)}, f32[64,128]{1,0:T(8,128)S(1)}, u32[]{:S(2)}, u32[]{:S(2)}) collective-permute-start(f32[64,128]{1,0:T(8,128)S(1)} %total.8.refs_0_), channel_id=1, source_target_pairs={{0,24},{2,26},{4,28},{6,30},{8,16},{10,18},{12,20},{14,22},{16,8},... | collective-permute-start | bytes 98312 | tf_op jit(solution)/shard_map/ppermute | solution.py:50
  21.6 4.8 %collective-permute-start.5 = (f32[64,128]{1,0:T(8,128)S(1)}, f32[64,128]{1,0:T(8,128)S(1)}, u32[]{:S(2)}, u32[]{:S(2)}) collective-permute-start(f32[64,128]{1,0:T(8,128)S(1)} %total.8.refs_0_), channel_id=1, source_target_pairs={{0,16},{2,18},{4,20},{6,22},{8,24},{10,26},{12,28},{14,30},{16,0},... | collective-permute-start | bytes 98312 | tf_op jit(solution)/shard_map/ppermute | solution.py:50
  21.6 4.8 %collective-permute-start.4 = (f32[64,128]{1,0:T(8,128)S(1)}, f32[64,128]{1,0:T(8,128)S(1)}, u32[]{:S(2)}, u32[]{:S(2)}) collective-permute-start(f32[64,128]{1,0:T(8,128)S(1)} %total.8.refs_0_), channel_id=1, source_target_pairs={{0,8},{2,10},{4,12},{6,14},{8,0},{10,2},{12,4},{14,6},{16,24},{18,... | collective-permute-start | bytes 98312 | tf_op jit(solution)/shard_map/ppermute | solution.py:50
  26.4 1.3 %collective-permute-start.7 = (f32[64,128]{1,0:T(8,128)S(1)}, f32[64,128]{1,0:T(8,128)S(1)}, u32[]{:S(2)}, u32[]{:S(2)}) collective-permute-start(f32[64,128]{1,0:T(8,128)S(1)} %total.9.own_ref), channel_id=1, source_target_pairs={{0,1},{1,0},{2,3},{3,2},{4,5},{5,4},{6,7},{7,6},{8,9},{9,8},{10,11... | collective-permute-start | bytes 98312 | tf_op jit(solution)/shard_map/ppermute | solution.py:50
  26.5 3.3 %copy-start.3 = (f32[128,3968]{1,0:T(8,128)}, f32[128,3968]{1,0:T(8,128)S(1)}, u32[]{:S(2)}) copy-start(f32[128,3968]{1,0:T(8,128)S(1)} %collective-permute-done.8.rest_0_) | copy-start | bytes 6094852
  29.8 1.6 %collective-permute-start.9 = (f32[512,128]{1,0:T(8,128)S(1)}, f32[512,128]{1,0:T(8,128)S(1)}, u32[]{:S(2)}, u32[]{:S(2)}) collective-permute-start(f32[512,128]{1,0:T(8,128)S(1)} %get-tuple-element.22), channel_id=1, source_target_pairs={{0,1},{1,0},{2,3},{3,2},{4,5},{5,4},{6,7},{7,6},{8,9},{9,8},{10,11... | collective-permute-start | bytes 786440 | tf_op jit(solution)/shard_map/ppermute | solution.py:50
  32.2 13.5 %all-to-all-start = ((f32[8,64,128]{2,1,0:T(8,128)}), f32[8,64,128]{2,1,0:T(8,128)S(1)}, u32[]{:S(2)}, u32[]{:S(2)}) async-start(f32[8,64,128]{2,1,0:T(8,128)} %bitcast.4), calls=%async_computation | async-start | bytes 524288 | tf_op jit(solution)/shard_map/all_to_all | solution.py:63
  45.7 4.4 %collective-permute-start.11 = (f32[64,128]{1,0:T(8,128)S(1)}, f32[64,128]{1,0:T(8,128)S(1)}, u32[]{:S(2)}, u32[]{:S(2)}) collective-permute-start(f32[64,128]{1,0:T(8,128)S(1)} %sum_parts.1.refs_1_.refs_0_), channel_id=1, source_target_pairs={{0,2},{2,0},{1,3},{3,1},{4,6},{6,4},{5,7},{7,5},{8,10},{10,8},{9,1... | collective-permute-start | bytes 98312 | tf_op jit(solution)/shard_map/ppermute | solution.py:50
  46.2 20.4 %collective-permute-start.13 = (f32[56,3968]{1,0:T(8,128)}, f32[56,3968]{1,0:T(8,128)}, u32[]{:S(2)}, u32[]{:S(2)}) collective-permute-start(f32[56,3968]{1,0:T(8,128)} %passed_on.8.refs_2_), channel_id=1, source_target_pairs={{0,2},{2,0},{1,3},{3,1},{4,6},{6,4},{5,7},{7,5},{8,10},{10,8},{9,1... | collective-permute-start | bytes 2666504 | tf_op jit(solution)/shard_map/ppermute | solution.py:50
  50.8 11.7 %all-to-all-start.1 = ((f32[8,64,128]{2,1,0:T(8,128)}), f32[8,64,128]{2,1,0:T(8,128)S(1)}, u32[]{:S(2)}, u32[]{:S(2)}) async-start(f32[8,64,128]{2,1,0:T(8,128)} %total.11), calls=%async_computation.1 | async-start | bytes 524288 | tf_op jit(solution)/shard_map/all_to_all | solution.py:63
  62.5 1.5 %collective-permute-start.12 = (f32[512,128]{1,0:T(8,128)S(1)}, f32[512,128]{1,0:T(8,128)S(1)}, u32[]{:S(2)}, u32[]{:S(2)}) collective-permute-start(f32[512,128]{1,0:T(8,128)S(1)} %passed_on.9.own_ref), channel_id=1, source_target_pairs={{0,1},{1,0},{2,3},{3,2},{4,5},{5,4},{6,7},{7,6},{8,9},{9,8},{10,11... | collective-permute-start | bytes 786440 | tf_op jit(solution)/shard_map/ppermute | solution.py:50
